TPU v7x, 128 devices: a whole 4x4x4 slice. The times are simulated.
128 devices in a mesh: dp: 16 (over y, x), context: 8 (over z, core).
Axes of the slice: x: 4, y: 4, z: 4, core: 2. Of those that a mesh axis runs over, the one named last changes fastest.
Arguments:
- tokens: bfloat16 [32768, 1024], P(('dp', 'context')), may hold values from -6 to 6
- segments: int32 [32768], P(('dp', 'context')), may hold values from 0 to 2, as said below
- cotangent: bfloat16 [32768, 1024], P(('dp', 'context')), may hold values from -6 to 6
- attention_gain: float32 [1024], replicated, may hold values from 0.5 to 1.5
- query_weight: bfloat16 [1024, 512], P('dp'), may hold values from -0.1875 to 0.1875
- key_matrix: bfloat16 [1024, 128], P('dp'), may hold values from -0.1875 to 0.1875
- value_matrix: bfloat16 [1024, 128], P('dp'), may hold values from -0.1875 to 0.1875
- attention_out: bfloat16 [512, 1024], P('dp'), may hold values from -3 to 3
- gate_weight: bfloat16 [1024, 1536], P('dp'), may hold values from -0.1875 to 0.1875
- mixer_weight: bfloat16 [1024, 1792], P('dp'), may hold values from -0.1875 to 0.1875
- step_weight: bfloat16 [1024, 24], P('dp'), may hold values from -0.1875 to 0.1875
- mixer_out: bfloat16 [1536, 1024], P('dp'), may hold values from -0.4375 to 0.4375
- conv_weight: float32 [4, 1792], replicated, may hold values from -3 to 3
- conv_bias: float32 [1792], replicated, may hold values from -3 to 3
- step_bias: float32 [24], replicated, may hold values from -4 to -1
- decay_log: float32 [24], replicated, may hold values from -3 to 1
- skip_gain: float32 [24], replicated, may hold values from 0.5 to 1.5
- feed_gain: float32 [1024], replicated, may hold values from 0.5 to 1.5
- feed_gate: bfloat16 [1024, 2048], P('dp'), may hold values from -0.1875 to 0.1875
- feed_up: bfloat16 [1024, 2048], P('dp'), may hold values from -0.1875 to 0.1875
- feed_down: bfloat16 [2048, 1024], P('dp'), may hold values from -0.125 to 0.125
Outputs:
- output: bfloat16 [32768, 1024], P(('dp', 'context'))
- grad_tokens: float32 [32768, 1024], P(('dp', 'context'))
- grad_attention_gain: float32 [1024], replicated
- grad_query_weight: float32 [1024, 512], P('dp')
- grad_key_weight: float32 [1024, 128], P('dp')
- grad_value_weight: float32 [1024, 128], P('dp')
- grad_attention_out: float32 [512, 1024], P('dp')
- grad_gate_weight: float32 [1024, 1536], P('dp')
- grad_mixer_weight: float32 [1024, 1792], P('dp')
- grad_step_weight: float32 [1024, 24], P('dp')
- grad_mixer_out: float32 [1536, 1024], P('dp')
- grad_conv_weight: float32 [4, 1792], replicated
- grad_conv_bias: float32 [1792], replicated
- grad_step_bias: float32 [24], replicated
- grad_decay_log: float32 [24], replicated
- grad_skip_gain: float32 [24], replicated
- grad_feed_gain: float32 [1024], replicated
- grad_feed_gate: float32 [1024, 2048], P('dp')
- grad_feed_up: float32 [1024, 2048], P('dp')
- grad_feed_down: float32 [2048, 1024], P('dp')
Inputs may be any that keep to these rules, and one draw needn't show every extreme that they name: `segments`: within each sequence of 2048 tokens the numbers never fall: document 0 ends within the sequence's first 256 tokens, document 2 begins within its last 256 tokens, and document 1 lies between.
All inputs are finite; a program needn't handle non-finite values.
Results may differ from a plain program's by a relative error of at most 0.02.
Values may be sent and summed in bfloat16 or wider, within the bound.
No kernel may reach another device: no remote copies, remote signals or barrier semaphores. Data moves between devices by JAX's collectives and lax.ppermute only.
A program may use at most 192 MiB of HBM per device.

v0:
```python
import math

import jax
import jax.numpy as jnp
from jax import lax
from jax.sharding import PartitionSpec as P

QUERY_HEADS = 8
KEY_VALUE_HEADS = 2
HEAD_WIDTH = 64
MH = 24
MP = 64
NS = 128


EPSILON = 1e-05
masked_fill = -1e30
attention_multiplier = 0.9375
mixer_multiplier = 0.2357
rotary_base = 100000000000.0


def from_behind(block, axis, distance):
    devices = range(lax.axis_size(axis))
    route = [(i - distance, i) for i in devices if i - distance in devices]
    return lax.ppermute(block, axis, route)


def carried_in(shard, axis, combine, identity, reverse):
    length, mine = (lax.axis_size(axis), lax.axis_index(axis))
    everything = jax.tree.map(
        lambda part, kind: lax.all_gather(part.astype(kind), axis),
        shard,
        (jnp.bfloat16, jnp.bfloat16),
    )
    start = jax.tree.map(
        lambda part, zero: jnp.broadcast_to(jnp.asarray(zero, part.dtype), part.shape),
        shard,
        identity,
    )

    def turn(k, before):
        at = length - 1 - k if reverse else k
        reached = at > mine if reverse else at < mine
        new = combine(
            before, jax.tree.map(lambda part, own: part[at].astype(own.dtype), everything, shard)
        )
        return jax.tree.map(lambda a, b: jnp.where(reached, a, b), new, before)

    return lax.fori_loop(0, length, turn, start)


def rms_norm(values, gain_vector):
    return (
        values
        * lax.rsqrt(jnp.mean(values * values, axis=-1, keepdims=True) + EPSILON)
        * gain_vector
    )


def rotary(values, places, direction):
    count_of_rows = values.shape[0]
    head_count = values.shape[1] // HEAD_WIDTH
    half_size = HEAD_WIDTH // 2
    frequency = rotary_base ** (-2.0 * jnp.arange(half_size, dtype=jnp.float32) / HEAD_WIDTH)
    angles = places[:, None] * frequency[None, :]
    cosine = jnp.cos(angles)[:, None, :]
    sine_part = direction * jnp.sin(angles)[:, None, :]
    per_head = values.reshape(count_of_rows, head_count, HEAD_WIDTH)
    front_half = per_head[:, :, :half_size]
    back_half = per_head[:, :, half_size:]
    turned = jnp.concatenate(
        [front_half * cosine - back_half * sine_part, back_half * cosine + front_half * sine_part],
        axis=-1,
    )
    return turned.reshape(count_of_rows, head_count * HEAD_WIDTH)


def mixer_inputs(
    extended, seg_extended, seg_own, conv_taps, conv_shift, step_raw, step_shift, decay_logs
):
    count_of_rows = seg_own.shape[0]
    mixed = conv_shift[None, :]
    for tap_index in range(conv_taps.shape[0]):
        same_doc = (seg_extended[tap_index : tap_index + count_of_rows] == seg_own).astype(
            jnp.float32
        )
        mixed = (
            mixed
            + conv_taps[tap_index][None, :]
            * extended[tap_index : tap_index + count_of_rows]
            * same_doc[:, None]
        )
    activated = jax.nn.silu(mixed)
    step_size = jax.nn.softplus(step_raw + step_shift[None, :])
    log_rate = step_size * (-jnp.exp(decay_logs))[None, :]
    return (activated, step_size, log_rate)


def decay_terms(log_rate, seg_own, seg_before):
    count_of_rows = log_rate.shape[0]
    running = jnp.cumsum(log_rate, axis=0)
    index_rows = jnp.arange(count_of_rows)
    allowed = (index_rows[:, None] >= index_rows[None, :]) & (seg_own[:, None] == seg_own[None, :])
    gaps = running.T[:, :, None] - running.T[:, None, :]
    within = jnp.exp(jnp.where(allowed[None], gaps, masked_fill))
    entry = jnp.exp(running) * (seg_own == seg_before).astype(jnp.float32)[:, None]
    leaving = (
        jnp.exp(running[-1][None, :] - running)
        * (seg_own == seg_own[-1]).astype(jnp.float32)[:, None]
    )
    carried = jnp.exp(running[-1]) * (seg_own[-1] == seg_before).astype(jnp.float32)
    return (within, entry, leaving, carried)


def attention_scores(rotated_queries, every_key, query_places, seg_own, seg_all):
    count_of_rows = rotated_queries.shape[0]
    count_of_keys = every_key.shape[0]
    heads_of_queries = rotated_queries.reshape(
        count_of_rows, KEY_VALUE_HEADS, QUERY_HEADS // KEY_VALUE_HEADS, HEAD_WIDTH
    )
    heads_of_keys = every_key.reshape(count_of_keys, KEY_VALUE_HEADS, HEAD_WIDTH)
    raw_scores = jnp.einsum(
        "rgqd,lgd->gqrl", heads_of_queries, heads_of_keys, preferred_element_type=jnp.float32
    ) * (1.0 / math.sqrt(HEAD_WIDTH))
    allowed = (jnp.arange(count_of_keys)[None, :] <= query_places[:, None]) & (
        seg_all[None, :] == seg_own[:, None]
    )
    return jnp.where(allowed[None, None], raw_scores, masked_fill)


def chain_forward(earlier, later):
    return (earlier[0] * later[0], later[0][:, None, None] * earlier[1] + later[1])


def chain_backward(earlier, later):
    return (earlier[0] * later[0], later[1] + later[0][:, None, None] * earlier[1])


def project(left, right):
    return jnp.dot(left, right, preferred_element_type=jnp.float32)


def input_grad(left, right):
    return jnp.einsum("rk,rj->kj", left, right, preferred_element_type=jnp.float32)


def back_through(grad_low, weight_full):
    return jnp.einsum("rj,kj->rk", grad_low, weight_full, preferred_element_type=jnp.float32)


def swiglu(gate_values, up_values):
    return jax.nn.silu(gate_values) * up_values


def gating(scan_values, gate_values):
    return scan_values * jax.nn.silu(gate_values)


def on_device(
    tokens,
    segments,
    cotangent,
    attention_gain,
    query_weight,
    key_matrix,
    value_matrix,
    attention_out,
    gate_weight,
    mixer_weight,
    step_weight,
    mixer_out,
    conv_weight,
    conv_bias,
    step_bias,
    decay_log,
    skip_gain,
    feed_gain,
    feed_gate,
    feed_up,
    feed_down,
):
    gathered = (
        lax.all_gather(query_weight, "dp", axis=0, tiled=True),
        lax.all_gather(key_matrix, "dp", axis=0, tiled=True),
        lax.all_gather(value_matrix, "dp", axis=0, tiled=True),
        lax.all_gather(attention_out, "dp", axis=0, tiled=True),
        lax.all_gather(gate_weight, "dp", axis=0, tiled=True),
        lax.all_gather(mixer_weight, "dp", axis=0, tiled=True),
        lax.all_gather(step_weight, "dp", axis=0, tiled=True),
        lax.all_gather(mixer_out, "dp", axis=0, tiled=True),
        lax.all_gather(feed_gate, "dp", axis=0, tiled=True),
        lax.all_gather(feed_up, "dp", axis=0, tiled=True),
        lax.all_gather(feed_down, "dp", axis=0, tiled=True),
    )
    (
        query_full,
        key_full,
        value_full,
        out_full,
        gate_full,
        mixer_full,
        step_full,
        mixer_out_full,
        ffn_gate_full,
        ffn_up_full,
        ffn_down_full,
    ) = gathered
    count_of_rows = tokens.shape[0]
    tap_count = conv_weight.shape[0]
    inner_width = MH * MP
    width_of_keys = KEY_VALUE_HEADS * HEAD_WIDTH
    block_index = lax.axis_index("context")
    query_places = block_index * count_of_rows + jnp.arange(count_of_rows, dtype=jnp.int32)
    place_float = query_places.astype(jnp.float32)
    seg_float = segments.astype(jnp.float32)
    seg_low = segments.astype(jnp.bfloat16)
    hidden_in = tokens.astype(jnp.float32)
    normed, norm_one_back = jax.vjp(rms_norm, hidden_in, attention_gain)
    normed_low = normed.astype(jnp.bfloat16)
    query_lin = project(normed_low, query_full)
    key_lin = project(normed_low, key_full)
    value_lin = project(normed_low, value_full)
    rotated_queries = rotary(query_lin, place_float, 1.0).astype(jnp.bfloat16)
    rotated_keys = rotary(key_lin, place_float, 1.0).astype(jnp.bfloat16)
    value_reduced = value_lin.astype(jnp.bfloat16)
    every_key, every_value, seg_all = (
        lax.all_gather(rotated_keys, "context", axis=0, tiled=True),
        lax.all_gather(value_reduced, "context", axis=0, tiled=True),
        lax.all_gather(seg_low, "context", axis=0, tiled=True),
    )
    heads_of_keys = every_key.reshape(-1, KEY_VALUE_HEADS, HEAD_WIDTH)
    heads_of_values = every_value.reshape(-1, KEY_VALUE_HEADS, HEAD_WIDTH)
    heads_of_queries = rotated_queries.reshape(
        count_of_rows, KEY_VALUE_HEADS, QUERY_HEADS // KEY_VALUE_HEADS, HEAD_WIDTH
    )
    scores = attention_scores(rotated_queries, every_key, query_places, seg_low, seg_all)
    top_score = jnp.max(scores, axis=-1, keepdims=True)
    exponent = jnp.exp(scores - top_score)
    totals = jnp.sum(exponent, axis=-1, keepdims=True)
    probs_low = (exponent / totals).astype(jnp.bfloat16)
    log_total = top_score + jnp.log(totals)
    attended = jnp.einsum(
        "gqrl,lgd->rgqd", probs_low, heads_of_values, preferred_element_type=jnp.float32
    )
    attended_low = attended.reshape(count_of_rows, QUERY_HEADS * HEAD_WIDTH).astype(jnp.bfloat16)
    attention_branch = project(attended_low, out_full)
    gate_lin = project(normed_low, gate_full)
    mixer_lin = project(normed_low, mixer_full)
    step_lin = project(normed_low, step_full)
    prev_rows, prev_segs = from_behind(
        (mixer_lin[count_of_rows - tap_count + 1 :], seg_float[count_of_rows - tap_count + 1 :]),
        "context",
        1,
    )
    extended = jnp.concatenate([prev_rows, mixer_lin], axis=0)
    seg_extended = jnp.concatenate([prev_segs, seg_float])
    seg_before = prev_segs[-1]

    def mixer_piece(ext_rows, conv_taps, conv_shift, step_raw, step_shift, decay_logs):
        return mixer_inputs(
            ext_rows,
            seg_extended,
            seg_float,
            conv_taps,
            conv_shift,
            step_raw,
            step_shift,
            decay_logs,
        )

    (activated, step_size, log_rate), mixer_back = jax.vjp(
        mixer_piece, extended, conv_weight, conv_bias, step_lin, step_bias, decay_log
    )
    mixer_x = activated[:, :inner_width].reshape(count_of_rows, MH, MP)
    bees = activated[:, inner_width : inner_width + NS].astype(jnp.bfloat16)
    seas = activated[:, inner_width + NS :].astype(jnp.bfloat16)
    inputs_low = (mixer_x * step_size[:, :, None]).astype(jnp.bfloat16)

    def decay_piece(rates):
        return decay_terms(rates, seg_float, seg_before)

    (within, entry, leaving, carried), decay_back = jax.vjp(decay_piece, log_rate)
    intersection = jnp.einsum("in,jn->ij", seas, bees, preferred_element_type=jnp.float32)
    mixing_low = (intersection[None] * within).astype(jnp.bfloat16)
    inner = jnp.einsum("hij,jhp->ihp", mixing_low, inputs_low, preferred_element_type=jnp.float32)
    weighted_low = (bees.astype(jnp.float32)[:, None, :] * leaving[:, :, None]).astype(jnp.bfloat16)
    local_state = jnp.einsum(
        "jhn,jhp->hnp", weighted_low, inputs_low, preferred_element_type=jnp.float32
    )
    identity = (jnp.ones((MH,), jnp.float32), jnp.zeros((MH, NS, MP), jnp.float32))
    incoming_decay, incoming = carried_in(
        (carried, local_state), "context", chain_forward, identity, False
    )
    incoming_low = incoming.astype(jnp.bfloat16)
    from_state = jnp.einsum("in,hnp->ihp", seas, incoming_low, preferred_element_type=jnp.float32)
    scanned = inner + from_state * entry[:, :, None] + skip_gain[None, :, None] * mixer_x
    gated, gating_back = jax.vjp(gating, scanned.reshape(count_of_rows, inner_width), gate_lin)
    gated_low = gated.astype(jnp.bfloat16)
    mixer_branch = project(gated_low, mixer_out_full)
    residual = hidden_in + attention_multiplier * attention_branch + mixer_multiplier * mixer_branch
    normed_two, norm_two_back = jax.vjp(rms_norm, residual, feed_gain)
    normed_two_low = normed_two.astype(jnp.bfloat16)
    ffn_gate_lin = project(normed_two_low, ffn_gate_full)
    ffn_up_lin = project(normed_two_low, ffn_up_full)
    hidden_act, swiglu_back = jax.vjp(swiglu, ffn_gate_lin, ffn_up_lin)
    hidden_low = hidden_act.astype(jnp.bfloat16)
    output = (residual + project(hidden_low, ffn_down_full)).astype(jnp.bfloat16)
    again = (
        lax.all_gather(query_weight, "dp", axis=0, tiled=True),
        lax.all_gather(key_matrix, "dp", axis=0, tiled=True),
        lax.all_gather(value_matrix, "dp", axis=0, tiled=True),
        lax.all_gather(attention_out, "dp", axis=0, tiled=True),
        lax.all_gather(gate_weight, "dp", axis=0, tiled=True),
        lax.all_gather(mixer_weight, "dp", axis=0, tiled=True),
        lax.all_gather(step_weight, "dp", axis=0, tiled=True),
        lax.all_gather(mixer_out, "dp", axis=0, tiled=True),
        lax.all_gather(feed_gate, "dp", axis=0, tiled=True),
        lax.all_gather(feed_up, "dp", axis=0, tiled=True),
        lax.all_gather(feed_down, "dp", axis=0, tiled=True),
    )
    (
        query_back,
        key_back,
        value_back,
        out_back,
        gate_back,
        mixer_in_back,
        step_back,
        mixer_out_back,
        ffn_gate_back,
        ffn_up_back,
        ffn_down_back,
    ) = again
    upstream = cotangent.astype(jnp.float32)
    grad_feed_down = input_grad(hidden_low, cotangent)
    d_hidden = back_through(cotangent, ffn_down_back)
    d_ffn_gate, d_ffn_up = swiglu_back(d_hidden)
    d_ffn_gate_low = d_ffn_gate.astype(jnp.bfloat16)
    d_ffn_up_low = d_ffn_up.astype(jnp.bfloat16)
    grad_feed_gate = input_grad(normed_two_low, d_ffn_gate_low)
    grad_feed_up = input_grad(normed_two_low, d_ffn_up_low)
    d_normed_two = back_through(d_ffn_gate_low, ffn_gate_back) + back_through(
        d_ffn_up_low, ffn_up_back
    )
    d_resid_norm, grad_feed_gain = norm_two_back(d_normed_two)
    d_residual = upstream + d_resid_norm
    d_attn_low = (attention_multiplier * d_residual).astype(jnp.bfloat16)
    d_mixer_low = (mixer_multiplier * d_residual).astype(jnp.bfloat16)
    grad_attention_out = input_grad(attended_low, d_attn_low)
    grad_mixer_out = input_grad(gated_low, d_mixer_low)
    attended_gradient = back_through(d_attn_low, out_back).astype(jnp.bfloat16)
    d_gated = back_through(d_mixer_low, mixer_out_back)
    scale_factor = 1.0 / math.sqrt(HEAD_WIDTH)
    scores_again = attention_scores(rotated_queries, every_key, query_places, seg_low, seg_all)
    probs_again = jnp.exp(scores_again - log_total)
    probs_again_low = probs_again.astype(jnp.bfloat16)
    output_heads_gradient = attended_gradient.reshape(
        count_of_rows, KEY_VALUE_HEADS, QUERY_HEADS // KEY_VALUE_HEADS, HEAD_WIDTH
    )
    d_probs = jnp.einsum(
        "rgqd,lgd->gqrl", output_heads_gradient, heads_of_values, preferred_element_type=jnp.float32
    )
    delta_sum = jnp.sum(probs_again * d_probs, axis=-1, keepdims=True)
    d_scores_low = (probs_again * (d_probs - delta_sum)).astype(jnp.bfloat16)
    d_query_rot = (
        jnp.einsum(
            "gqrl,lgd->rgqd", d_scores_low, heads_of_keys, preferred_element_type=jnp.float32
        ).reshape(count_of_rows, QUERY_HEADS * HEAD_WIDTH)
        * scale_factor
    )
    d_keys = (
        jnp.einsum(
            "gqrl,rgqd->lgd", d_scores_low, heads_of_queries, preferred_element_type=jnp.float32
        ).reshape(count_of_rows * lax.axis_size("context"), width_of_keys)
        * scale_factor
    )
    d_values = jnp.einsum(
        "gqrl,rgqd->lgd", probs_again_low, output_heads_gradient, preferred_element_type=jnp.float32
    ).reshape(count_of_rows * lax.axis_size("context"), width_of_keys)
    key_grads = lax.psum_scatter(
        jnp.concatenate([d_keys, d_values], axis=1).astype(jnp.bfloat16),
        "context",
        scatter_dimension=0,
        tiled=True,
    ).astype(jnp.float32)
    d_query_low = rotary(d_query_rot, place_float, -1.0).astype(jnp.bfloat16)
    d_key_low = rotary(key_grads[:, :width_of_keys], place_float, -1.0).astype(jnp.bfloat16)
    d_value_low = key_grads[:, width_of_keys:].astype(jnp.bfloat16)
    d_scan_flat, d_gate_lin = gating_back(d_gated)
    d_scan_low = d_scan_flat.reshape(count_of_rows, MH, MP).astype(jnp.bfloat16)
    d_scan = d_scan_low.astype(jnp.float32)
    grad_skip_gain = jnp.sum(d_scan * mixer_x, axis=(0, 2))
    d_mixer_x = skip_gain[None, :, None] * d_scan
    d_entry = jnp.sum(d_scan * from_state, axis=2)
    d_from_low = (d_scan * entry[:, :, None]).astype(jnp.bfloat16)
    d_seas = jnp.einsum("ihp,hnp->in", d_from_low, incoming_low, preferred_element_type=jnp.float32)
    d_incoming = jnp.einsum("in,ihp->hnp", seas, d_from_low, preferred_element_type=jnp.float32)
    d_mixing = jnp.einsum(
        "ihp,jhp->hij", d_scan_low, inputs_low, preferred_element_type=jnp.float32
    )
    d_inputs = jnp.einsum(
        "hij,ihp->jhp", mixing_low, d_scan_low, preferred_element_type=jnp.float32
    )
    d_intersection_low = jnp.sum(d_mixing * within, axis=0).astype(jnp.bfloat16)
    d_within = d_mixing * intersection[None]
    d_seas = d_seas + jnp.einsum(
        "ij,jn->in", d_intersection_low, bees, preferred_element_type=jnp.float32
    )
    d_bees = jnp.einsum("ij,in->jn", d_intersection_low, seas, preferred_element_type=jnp.float32)
    outgoing_decay, d_outgoing = carried_in(
        (carried, d_incoming), "context", chain_backward, identity, True
    )
    d_state_low = d_outgoing.astype(jnp.bfloat16)
    d_carried = jnp.sum(d_outgoing * incoming, axis=(1, 2))
    d_weighted = jnp.einsum(
        "jhp,hnp->jhn", inputs_low, d_state_low, preferred_element_type=jnp.float32
    )
    d_inputs = d_inputs + jnp.einsum(
        "jhn,hnp->jhp", weighted_low, d_state_low, preferred_element_type=jnp.float32
    )
    d_bees = d_bees + jnp.sum(d_weighted * leaving[:, :, None], axis=1)
    d_leaving = jnp.sum(d_weighted * bees.astype(jnp.float32)[:, None, :], axis=2)
    (d_rate,) = decay_back((d_within, d_entry, d_leaving, d_carried))
    d_mixer_x = d_mixer_x + d_inputs * step_size[:, :, None]
    d_step = jnp.sum(d_inputs * mixer_x, axis=2)
    d_activated = jnp.concatenate(
        [d_mixer_x.reshape(count_of_rows, inner_width), d_bees, d_seas], axis=1
    )
    d_extended, grad_conv_weight, grad_conv_bias, d_step_lin, grad_step_bias, grad_decay_log = (
        mixer_back((d_activated, d_step, d_rate))
    )
    rim_back = from_behind(d_extended[: tap_count - 1], "context", -1)
    d_mixer_lin = d_extended[tap_count - 1 :] + jnp.pad(
        rim_back, ((count_of_rows - tap_count + 1, 0), (0, 0))
    )
    d_gate_low = d_gate_lin.astype(jnp.bfloat16)
    d_mixer_in_low = d_mixer_lin.astype(jnp.bfloat16)
    d_step_low = d_step_lin.astype(jnp.bfloat16)
    grad_query_weight = input_grad(normed_low, d_query_low)
    grad_key_weight = input_grad(normed_low, d_key_low)
    grad_value_weight = input_grad(normed_low, d_value_low)
    grad_gate_weight = input_grad(normed_low, d_gate_low)
    grad_mixer_weight = input_grad(normed_low, d_mixer_in_low)
    grad_step_weight = input_grad(normed_low, d_step_low)
    d_normed = (
        back_through(d_query_low, query_back)
        + back_through(d_key_low, key_back)
        + back_through(d_value_low, value_back)
        + back_through(d_gate_low, gate_back)
        + back_through(d_mixer_in_low, mixer_in_back)
        + back_through(d_step_low, step_back)
    )
    d_tokens_norm, grad_attention_gain = norm_one_back(d_normed)
    grad_tokens = d_residual + d_tokens_norm
    pieces = (
        lax.psum_scatter(
            grad_query_weight.astype(jnp.bfloat16), "dp", scatter_dimension=0, tiled=True
        ).astype(jnp.float32),
        lax.psum_scatter(
            grad_key_weight.astype(jnp.bfloat16), "dp", scatter_dimension=0, tiled=True
        ).astype(jnp.float32),
        lax.psum_scatter(
            grad_value_weight.astype(jnp.bfloat16), "dp", scatter_dimension=0, tiled=True
        ).astype(jnp.float32),
        lax.psum_scatter(
            grad_attention_out.astype(jnp.bfloat16), "dp", scatter_dimension=0, tiled=True
        ).astype(jnp.float32),
        lax.psum_scatter(
            grad_gate_weight.astype(jnp.bfloat16), "dp", scatter_dimension=0, tiled=True
        ).astype(jnp.float32),
        lax.psum_scatter(
            grad_mixer_weight.astype(jnp.bfloat16), "dp", scatter_dimension=0, tiled=True
        ).astype(jnp.float32),
        lax.psum_scatter(
            grad_step_weight.astype(jnp.bfloat16), "dp", scatter_dimension=0, tiled=True
        ).astype(jnp.float32),
        lax.psum_scatter(
            grad_mixer_out.astype(jnp.bfloat16), "dp", scatter_dimension=0, tiled=True
        ).astype(jnp.float32),
        lax.psum_scatter(
            grad_feed_gate.astype(jnp.bfloat16), "dp", scatter_dimension=0, tiled=True
        ).astype(jnp.float32),
        lax.psum_scatter(
            grad_feed_up.astype(jnp.bfloat16), "dp", scatter_dimension=0, tiled=True
        ).astype(jnp.float32),
        lax.psum_scatter(
            grad_feed_down.astype(jnp.bfloat16), "dp", scatter_dimension=0, tiled=True
        ).astype(jnp.float32),
    )
    summed = (
        lax.psum(pieces[0].astype(jnp.bfloat16), "context").astype(jnp.float32),
        lax.psum(pieces[1].astype(jnp.bfloat16), "context").astype(jnp.float32),
        lax.psum(pieces[2].astype(jnp.bfloat16), "context").astype(jnp.float32),
        lax.psum(pieces[3].astype(jnp.bfloat16), "context").astype(jnp.float32),
        lax.psum(pieces[4].astype(jnp.bfloat16), "context").astype(jnp.float32),
        lax.psum(pieces[5].astype(jnp.bfloat16), "context").astype(jnp.float32),
        lax.psum(pieces[6].astype(jnp.bfloat16), "context").astype(jnp.float32),
        lax.psum(pieces[7].astype(jnp.bfloat16), "context").astype(jnp.float32),
        lax.psum(pieces[8].astype(jnp.bfloat16), "context").astype(jnp.float32),
        lax.psum(pieces[9].astype(jnp.bfloat16), "context").astype(jnp.float32),
        lax.psum(pieces[10].astype(jnp.bfloat16), "context").astype(jnp.float32),
    )
    small = lax.psum(
        (
            grad_attention_gain,
            grad_conv_weight,
            grad_conv_bias,
            grad_step_bias,
            grad_decay_log,
            grad_skip_gain,
            grad_feed_gain,
        ),
        ("dp", "context"),
    )
    return (
        output,
        grad_tokens,
        small[0],
        summed[0],
        summed[1],
        summed[2],
        summed[3],
        summed[4],
        summed[5],
        summed[6],
        summed[7],
        small[1],
        small[2],
        small[3],
        small[4],
        small[5],
        small[6],
        summed[8],
        summed[9],
        summed[10],
    )


def solution(mesh):
    return jax.shard_map(
        on_device,
        mesh=mesh,
        in_specs=(
            P(("dp", "context"), None),
            P(("dp", "context")),
            P(("dp", "context"), None),
            P(),
            P("dp", None),
            P("dp", None),
            P("dp", None),
            P("dp", None),
            P("dp", None),
            P("dp", None),
            P("dp", None),
            P("dp", None),
            P(),
            P(),
            P(),
            P(),
            P(),
            P(),
            P("dp", None),
            P("dp", None),
            P("dp", None),
        ),
        out_specs=(
            P(("dp", "context"), None),
            P(("dp", "context"), None),
            P(),
            P("dp", None),
            P("dp", None),
            P("dp", None),
            P("dp", None),
            P("dp", None),
            P("dp", None),
            P("dp", None),
            P("dp", None),
            P(),
            P(),
            P(),
            P(),
            P(),
            P(),
            P("dp", None),
            P("dp", None),
            P("dp", None),
        ),
        check_vma=False,
    )
```

profile of v0, /device:TPU:0, one launch (start us, length us, event | category | flops | bytes accessed | tf_op | source)
XLA Modules:
  0.0 1473.1 jit_solution(3567512948974202765)
XLA Ops:
  13.0 24.5 %all-gather.3 = bf16[16,64,24]{1,2,0:T(8,128)(2,1)S(1)} all-gather(bf16[1,64,24]{1,2,0:T(8,128)(2,1)} %bitcast.330), channel_id=1, replica_groups=mesh['dp'=16,'context'=8] {'dp'}, dimensions={0}, use_global_device_ids=true | all-gather | bytes 52224 | tf_op jit(solution)/shard_map/all_gather | solution.py:190
  43.6 18.7 %all-gather.20.cloned.1.call-done = bf16[1024,1792]{1,0:T(8,128)(2,1)} async-done(((bf16[64,1792]{1,0:T(8,128)(2,1)}), bf16[1024,1792]{1,0:T(8,128)(2,1)}) %all-gather.20.cloned.1.call-update) | async-done | bytes 3670032 | tf_op jit(solution)/shard_map/all_gather | solution.py:189
  81.9 23.6 %all_gather.71 = bf16[1024,128]{1,0:T(8,128)(2,1)S(1)} all-gather(bf16[64,128]{1,0:T(8,128)(2,1)S(1)} %copy-done.116), channel_id=1, replica_groups=mesh['dp'=16,'context'=8] {'dp'}, dimensions={0}, use_global_device_ids=true | all-gather | bytes 278528 | tf_op jit(solution)/shard_map/all_gather | solution.py:186
  106.6 15.8 %all_gather.72 = bf16[2048,128]{1,0:T(8,128)(2,1)S(1)} all-gather(bf16[256,128]{1,0:T(8,128)(2,1)S(1)} %convolution_convert_fusion.12), channel_id=1, replica_groups=mesh['dp'=16,'context'=8] {'context'}, dimensions={0}, use_global_device_ids=true | all-gather | bytes 589824 | tf_op jit(solution)/shard_map/all_gather | solution.py:229
  123.5 22.1 %all_gather.74 = bf16[1024,128]{1,0:T(8,128)(2,1)S(1)} all-gather(bf16[64,128]{1,0:T(8,128)(2,1)S(1)} %copy-done.117), channel_id=1, replica_groups=mesh['dp'=16,'context'=8] {'dp'}, dimensions={0}, use_global_device_ids=true | all-gather | bytes 278528 | tf_op jit(solution)/shard_map/all_gather | solution.py:185
  146.8 13.1 all_gather.75
  159.9 10.7 all-gather.2
  172.7 8.3 all-gather.4
  183.5 7.2 fusion.155
  190.7 8.1 fusion.5
  198.9 7.4 fusion.70
  208.2 22.8 %while.30 = (s32[]{:T(128)}, f32[24,128,64]{2,1,0:T(8,128)S(1)}, s32[]{:T(128)}, bf16[8,24]{1,0:T(8,128)(2,1)}, bf16[8,24,128,64]{2,3,1,0:T(8,128)(2,1)}, /*index=5*/s32[]{:T(128)}, s32[]{:T(128)}) while((s32[]{:T(128)}, f32[24,128,64]{2,1,0:T(8,128)S(1)}, s32[]{:T(128)}, bf16[8,24]{1,0:T(8,128)(2,1)}, ...), condition=%wide.region_6.7_spmd.clone, body=%wide.region_5.6_spmd.clone.sunk | while | flops 983068 | bytes 3539297 | solution.py:50
  232.9 3.5 fusion.55
  239.5 4.6 multiply_convert_fusion.9
  244.1 4.2 convolution_multiply_fusion
  248.3 29.7 %all-gather.18.cloned.1.call-done = bf16[512,1024]{1,0:T(8,128)(2,1)} async-done(((bf16[32,1024]{1,0:T(8,128)(2,1)}), bf16[512,1024]{1,0:T(8,128)(2,1)}) %all-gather.18.cloned.1.call-update) | async-done | bytes 1048592 | tf_op jit(solution)/shard_map/all_gather | solution.py:187
  281.3 49.5 %all-gather.26.cloned.1.call-done = bf16[1024,2048]{1,0:T(8,128)(2,1)} async-done(((bf16[64,2048]{1,0:T(8,128)(2,1)}), bf16[1024,2048]{1,0:T(8,128)(2,1)}) %all-gather.26.cloned.1.call-update) | async-done | bytes 4194320 | tf_op jit(solution)/shard_map/all_gather | solution.py:192
  330.9 5.0 fusion.156
  335.8 48.3 %all-gather.28.cloned.1.call-done = bf16[1024,2048]{1,0:T(8,128)(2,1)} async-done(((bf16[64,2048]{1,0:T(8,128)(2,1)}), bf16[1024,2048]{1,0:T(8,128)(2,1)}) %all-gather.28.cloned.1.call-update) | async-done | bytes 4194320 | tf_op jit(solution)/shard_map/all_gather | solution.py:193
  384.2 4.9 fusion.157
  389.1 48.4 %all-gather.30.cloned.1.call-done = bf16[2048,1024]{1,0:T(8,128)(2,1)} async-done(((bf16[128,1024]{1,0:T(8,128)(2,1)}), bf16[2048,1024]{1,0:T(8,128)(2,1)}) %all-gather.30.cloned.1.call-update) | async-done | bytes 4194320 | tf_op jit(solution)/shard_map/all_gather | solution.py:194
  437.5 6.8 multiply_convert_fusion.6
  451.7 3.5 multiply_reduce_fusion.5
  463.6 13.7 fusion.2
  480.6 10.5 fusion.4
  491.2 6.8 fusion.34
  498.0 3.6 fusion.31
  503.8 5.1 convolution_multiply_fusion.2
  512.8 3.9 convolution_convert_fusion.1
  532.5 3.4 convolution_convert_fusion.2
  535.9 5.3 fusion.12
  546.1 38.3 %while.31 = (s32[]{:T(128)}, f32[24,128,64]{2,1,0:T(8,128)}, s32[]{:T(128)}, bf16[8,24,128,64]{2,3,1,0:T(8,128)(2,1)}, bf16[8,24]{1,0:T(8,128)(2,1)}, /*index=5*/s32[]{:T(128)}, s32[]{:T(128)}, s32[]{:T(128)}, s32[]{:T(128)}) while((s32[]{:T(128)}, f32[24,128,64]{2,1,0:T(8,128)}, s32[]{:T(128)}, ...), condition=%wide.region_12.13_spmd.clone, body=%wide.region_11.12_spmd.clone.sunk | while | flops 983072 | bytes 3539359 | solution.py:50
  589.4 5.3 fusion.51
  599.0 6.5 multiply_reduce_fusion.3
  617.3 4.0 fusion.160
  638.8 47.1 %reduce-scatter.23.cloned.1.call-done = bf16[32,1024]{1,0:T(8,128)(2,1)} async-done(((bf16[512,1024]{1,0:T(8,128)(2,1)}), bf16[32,1024]{1,0:T(8,128)(2,1)}) %reduce-scatter.23.cloned.1.call-update) | async-done | bytes 65552 | tf_op jit(solution)/shard_map/reduce_scatter | solution.py:466
  685.9 78.2 %reduce-scatter.25.cloned.1.call-done = bf16[64,1536]{1,0:T(8,128)(2,1)} async-done(((bf16[1024,1536]{1,0:T(8,128)(2,1)}), bf16[64,1536]{1,0:T(8,128)(2,1)}) %reduce-scatter.25.cloned.1.call-update) | async-done | bytes 196624 | tf_op jit(solution)/shard_map/reduce_scatter | solution.py:469
  764.1 78.2 %reduce-scatter.29.cloned.1.call-done = bf16[96,1024]{1,0:T(8,128)(2,1)} async-done(((bf16[1536,1024]{1,0:T(8,128)(2,1)}), bf16[96,1024]{1,0:T(8,128)(2,1)}) %reduce-scatter.29.cloned.1.call-update) | async-done | bytes 196624 | tf_op jit(solution)/shard_map/reduce_scatter | solution.py:478
  842.3 80.1 %reduce-scatter.31.cloned.1.call-done = bf16[64,2048]{1,0:T(8,128)(2,1)} async-done(((bf16[1024,2048]{1,0:T(8,128)(2,1)}), bf16[64,2048]{1,0:T(8,128)(2,1)}) %reduce-scatter.31.cloned.1.call-update) | async-done | bytes 262160 | tf_op jit(solution)/shard_map/reduce_scatter | solution.py:481
  922.3 80.4 %reduce-scatter.33.cloned.1.call-done = bf16[64,2048]{1,0:T(8,128)(2,1)} async-done(((bf16[1024,2048]{1,0:T(8,128)(2,1)}), bf16[64,2048]{1,0:T(8,128)(2,1)}) %reduce-scatter.33.cloned.1.call-update) | async-done | bytes 262160 | tf_op jit(solution)/shard_map/reduce_scatter | solution.py:484
  1002.7 80.1 %reduce-scatter.35.cloned.1.call-done = bf16[128,1024]{1,0:T(8,128)(2,1)} async-done(((bf16[2048,1024]{1,0:T(8,128)(2,1)}), bf16[128,1024]{1,0:T(8,128)(2,1)}) %reduce-scatter.35.cloned.1.call-update) | async-done | bytes 262160 | tf_op jit(solution)/shard_map/reduce_scatter | solution.py:487
  1082.8 79.7 %reduce-scatter.27.cloned.1.call-done = bf16[64,1792]{1,0:T(8,128)(2,1)} async-done(((bf16[1024,1792]{1,0:T(8,128)(2,1)}), bf16[64,1792]{1,0:T(8,128)(2,1)}) %reduce-scatter.27.cloned.1.call-update) | async-done | bytes 229392 | tf_op jit(solution)/shard_map/reduce_scatter | solution.py:472
  1162.6 5.0 fusion.72
  1167.6 65.4 %all-reduce.11 = (f32[1024]{0:T(1024)}, f32[4,1792]{1,0:T(4,128)}, f32[1792]{0:T(1024)}, f32[24]{0:T(128)}, f32[24]{0:T(128)}, /*index=5*/f32[24]{0:T(128)}, f32[1024]{0:T(1024)}) all-reduce(f32[1024]{0:T(1024)S(1)} %get-tuple-element.346, f32[4,1792]{1,0:T(4,128)S(1)} %pad_add_fusion.2, ...), channel_id=1, replica_groups=mesh['dp'=16,'context'=8] {'dp','context'}, use_global_device_ids=true, to_apply=%region_26.27 | all-reduce | flops 11080 | bytes 88640 | tf_op jit(solution)/shard_map/psum | solution.py:504
  1238.4 74.3 %reduce-scatter.19.cloned.1.call-done = bf16[64,128]{1,0:T(8,128)(2,1)} async-done(((bf16[1024,128]{1,0:T(8,128)(2,1)}), bf16[64,128]{1,0:T(8,128)(2,1)}) %reduce-scatter.19.cloned.1.call-update) | async-done | bytes 16400 | tf_op jit(solution)/shard_map/reduce_scatter | solution.py:460
  1312.7 75.4 %reduce-scatter.21.cloned.1.call-done = bf16[64,128]{1,0:T(8,128)(2,1)} async-done(((bf16[1024,128]{1,0:T(8,128)(2,1)}), bf16[64,128]{1,0:T(8,128)(2,1)}) %reduce-scatter.21.cloned.1.call-update) | async-done | bytes 16400 | tf_op jit(solution)/shard_map/reduce_scatter | solution.py:463
  1388.1 24.6 %all-reduce.12 = (bf16[64,128]{1,0:T(8,128)(2,1)S(1)}, bf16[64,128]{1,0:T(8,128)(2,1)S(1)}, bf16[64,24]{0,1:T(8,128)(2,1)S(1)}) all-reduce(bf16[64,128]{1,0:T(8,128)(2,1)} %reduce-scatter.19.cloned.1.call-done, bf16[64,128]{1,0:T(8,128)(2,1)} %reduce-scatter.21.cloned.1.call-done, ...), channel_id=1, replica_groups=mesh['dp'=16,'context'=8] {'context'}, use_global_device_ids=true, to_apply=%region_30.31 | all-reduce | flops 17920 | bytes 71680 | tf_op jit(solution)/shard_map/psum | solution.py:493
  1414.5 40.8 %all-reduce.16.cloned.1.call-done = (bf16[64,512]{1,0:T(8,128)(2,1)}, bf16[32,1024]{1,0:T(8,128)(2,1)}, bf16[64,1536]{1,0:T(8,128)(2,1)}, bf16[64,1792]{1,0:T(8,...) async-done(((bf16[64,512]{1,0:T(8,128)(2,1)}, bf16[32,1024]{1,0:T(8,128)(2,1)}, ...) | async-done | bytes 1540112 | tf_op jit(solution)/shard_map/psum | solution.py:492
  (538 shorter events, 210.2 us)
Async XLA Ops:
  7.2 35.0 %copy-start.125 = (s32[256]{0:T(256)S(1)}, s32[256]{0:T(256)}, u32[]{:S(2)}) copy-start(s32[256]{0:T(256)} %param.26) | copy-start | bytes 3076
  7.2 55.1 %copy-start.3 = (bf16[256,1024]{1,0:T(8,128)(2,1)S(1)}, bf16[256,1024]{1,0:T(8,128)(2,1)}, u32[]{:S(2)}) copy-start(bf16[256,1024]{1,0:T(8,128)(2,1)} %param.25) | copy-start | bytes 1572868
  7.2 55.1 %copy-start.70 = (f32[1024]{0:T(1024)S(1)}, f32[1024]{0:T(1024)}, u32[]{:S(2)}) copy-start(f32[1024]{0:T(1024)} %param.28) | copy-start | bytes 12292
  7.2 55.1 %all-gather.20.cloned.1.call-start = ((), (), s32[]{:S(2)}) async-start(), calls=%async_computation.14 | async-start | bytes 3899392 | tf_op jit(solution)/shard_map/all_gather | solution.py:189
  8.0 173.6 %all-gather.16.cloned.1.call-start = ((), (), s32[]{:S(2)}) async-start(), calls=%async_computation.12 | async-start | bytes 1114112 | tf_op jit(solution)/shard_map/all_gather | solution.py:184
  8.8 32.7 %collective-permute-start.1 = (f32[3]{0:T(128)S(1)}, f32[3]{0:T(128)S(1)}, u32[]{:S(2)}, u32[]{:S(2)}) collective-permute-start(f32[3]{0:T(128)S(1)} %slice.115), channel_id=1, source_target_pairs={{0,1},{1,2},{2,3},{3,4},{4,5},{5,6},{6,7},{8,9},{9,10},{10,11},{11... | collective-permute-start | bytes 44 | tf_op jit(solution)/shard_map/ppermute | solution.py:26
  10.1 198.0 %all-gather.32.cloned.1.call-start = ((), (), s32[]{:S(2)}) async-start(), calls=%async_computation.31 | async-start | bytes 3538944 | tf_op jit(solution)/shard_map/all_gather | solution.py:32
  12.0 30.2 %copy-start.119 = (f32[256]{0:T(256)}, f32[256]{0:T(256)S(1)}, u32[]{:S(2)}) copy-start(f32[256]{0:T(256)S(1)} %fusion.75) | copy-start | bytes 3076
  13.0 54.8 %copy-start.80 = (f32[1792]{0:T(1024)}, f32[1792]{0:T(1024)S(1)}, u32[]{:S(2)}) copy-start(f32[1792]{0:T(1024)S(1)} %get-tuple-element.348) | copy-start | bytes 21508
  13.0 54.8 %copy-start.82 = (f32[1792]{0:T(1024)}, f32[1792]{0:T(1024)S(1)}, u32[]{:S(2)}) copy-start(f32[1792]{0:T(1024)S(1)} %get-tuple-element.349) | copy-start | bytes 21508
  13.0 54.8 %copy-start.84 = (f32[1792]{0:T(1024)}, f32[1792]{0:T(1024)S(1)}, u32[]{:S(2)}) copy-start(f32[1792]{0:T(1024)S(1)} %get-tuple-element.350) | copy-start | bytes 21508
  13.0 54.8 %copy-start.86 = (f32[1792]{0:T(1024)}, f32[1792]{0:T(1024)S(1)}, u32[]{:S(2)}) copy-start(f32[1792]{0:T(1024)S(1)} %get-tuple-element.351) | copy-start | bytes 21508
  37.7 27.9 %copy-start.66 = (bf16[1024,24]{0,1:T(8,128)(2,1)}, bf16[1024,24]{0,1:T(8,128)(2,1)S(1)}, u32[]{:S(2)}) copy-start(bf16[1024,24]{0,1:T(8,128)(2,1)S(1)} %reshape.484) | copy-start | bytes 147460
  39.8 35.8 %copy-start.98 = (f32[256,24]{0,1:T(8,128)}, f32[256,24]{0,1:T(8,128)S(1)}, u32[]{:S(2)}) copy-start(f32[256,24]{0,1:T(8,128)S(1)} %get-tuple-element.433) | copy-start | bytes 73732
  40.5 26.5 %copy-start.49 = (f32[24,2,128]{2,0,1:T(8,128)}, f32[24,2,128]{2,0,1:T(8,128)S(1)}, u32[]{:S(2)}) copy-start(f32[24,2,128]{2,0,1:T(8,128)S(1)} %reduce-window.14) | copy-start | bytes 73732
  40.7 26.3 %copy-start.96 = (f32[24,2]{0,1:T(2,128)}, f32[24,2]{0,1:T(2,128)S(1)}, u32[]{:S(2)}) copy-start(f32[24,2]{0,1:T(2,128)S(1)} %slice.128) | copy-start | bytes 580
  41.4 131.1 %copy-start.68 = (f32[256,24]{0,1:T(8,128)}, f32[256,24]{0,1:T(8,128)S(1)}, u32[]{:S(2)}) copy-start(f32[256,24]{0,1:T(8,128)S(1)} %get-tuple-element.421) | copy-start | bytes 73732
  65.6 2.2 collective-permute-start
  77.1 162.4 %all-gather.22.cloned.1.call-start = ((), (), s32[]{:S(2)}) async-start(), calls=%async_computation.15 | async-start | bytes 3342336 | tf_op jit(solution)/shard_map/all_gather | solution.py:188
  77.7 166.5 %all-gather.24.cloned.1.call-start = ((), (), s32[]{:S(2)}) async-start(), calls=%async_computation.16 | async-start | bytes 3342336 | tf_op jit(solution)/shard_map/all_gather | solution.py:191
  78.3 199.7 %all-gather.18.cloned.1.call-start = ((), (), s32[]{:S(2)}) async-start(), calls=%async_computation.13 | async-start | bytes 1114112 | tf_op jit(solution)/shard_map/all_gather | solution.py:187
  78.9 252.0 %all-gather.26.cloned.1.call-start = ((), (), s32[]{:S(2)}) async-start(), calls=%async_computation.17 | async-start | bytes 4456448 | tf_op jit(solution)/shard_map/all_gather | solution.py:192
  79.6 43.9 %copy-start.117 = (bf16[64,128]{1,0:T(8,128)(2,1)S(1)}, bf16[64,128]{1,0:T(8,128)(2,1)}, u32[]{:S(2)}) copy-start(bf16[64,128]{1,0:T(8,128)(2,1)} %param.30) | copy-start | bytes 49156
  79.6 304.5 %all-gather.28.cloned.1.call-start = ((), (), s32[]{:S(2)}) async-start(), calls=%async_computation.18 | async-start | bytes 4456448 | tf_op jit(solution)/shard_map/all_gather | solution.py:193
  80.4 357.1 %all-gather.30.cloned.1.call-start = ((), (), s32[]{:S(2)}) async-start(), calls=%async_computation.19 | async-start | bytes 4456448 | tf_op jit(solution)/shard_map/all_gather | solution.py:194
  81.1 465.0 %all-gather.34.cloned.1.call-start = ((), (), s32[]{:S(2)}) async-start(), calls=%async_computation.32 | async-start | bytes 3538944 | tf_op jit(solution)/shard_map/all_gather | solution.py:32
  146.7 36.6 %copy-start.51 = (f32[256,32]{0,1:T(8,128)}, f32[256,32]{0,1:T(8,128)S(1)}, u32[]{:S(2)}) copy-start(f32[256,32]{0,1:T(8,128)S(1)} %get-tuple-element.427) | copy-start | bytes 98308
  206.3 71.7 %copy-start.41 = (bf16[2,64,4,256]{3,1,2,0:T(8,128)(2,1)}, bf16[2,64,4,256]{3,1,2,0:T(8,128)(2,1)S(1)}, u32[]{:S(2)}) copy-start(bf16[2,64,4,256]{3,1,2,0:T(8,128)(2,1)S(1)} %fusion.70) | copy-start | bytes 786436
  280.2 165.3 %copy-start.6 = (f32[256,1024]{1,0:T(8,128)}, f32[256,1024]{1,0:T(8,128)S(1)}, u32[]{:S(2)}) copy-start(f32[256,1024]{1,0:T(8,128)S(1)} %get-tuple-element.440) | copy-start | bytes 3145732
  451.0 65.8 %copy-start.1 = (f32[256,1024]{1,0:T(8,128)}, f32[256,1024]{1,0:T(8,128)S(1)}, u32[]{:S(2)}) copy-start(f32[256,1024]{1,0:T(8,128)S(1)} %fusion.73) | copy-start | bytes 3145732
  459.8 163.6 %reduce-scatter.15.cloned.1.call-start = ((), (), s32[]{:S(2)}) async-start(), calls=%async_computation.20 | async-start | bytes 1179648 | tf_op jit(solution)/shard_map/reduce_scatter | solution.py:381
  503.8 135.0 %reduce-scatter.17.cloned.1.call-start = ((), (), s32[]{:S(2)}) async-start(), calls=%async_computation.21 | async-start | bytes 1114112 | tf_op jit(solution)/shard_map/reduce_scatter | solution.py:457
  511.3 174.6 %reduce-scatter.23.cloned.1.call-start = ((), (), s32[]{:S(2)}) async-start(), calls=%async_computation.24 | async-start | bytes 1114112 | tf_op jit(solution)/shard_map/reduce_scatter | solution.py:466
  512.8 251.3 %reduce-scatter.25.cloned.1.call-start = ((), (), s32[]{:S(2)}) async-start(), calls=%async_computation.25 | async-start | bytes 3342336 | tf_op jit(solution)/shard_map/reduce_scatter | solution.py:469
  516.7 325.5 %reduce-scatter.29.cloned.1.call-start = ((), (), s32[]{:S(2)}) async-start(), calls=%async_computation.27 | async-start | bytes 3342336 | tf_op jit(solution)/shard_map/reduce_scatter | solution.py:478
  520.6 401.8 %reduce-scatter.31.cloned.1.call-start = ((), (), s32[]{:S(2)}) async-start(), calls=%async_computation.28 | async-start | bytes 4456448 | tf_op jit(solution)/shard_map/reduce_scatter | solution.py:481
  525.2 477.5 %reduce-scatter.33.cloned.1.call-start = ((), (), s32[]{:S(2)}) async-start(), calls=%async_computation.29 | async-start | bytes 4456448 | tf_op jit(solution)/shard_map/reduce_scatter | solution.py:484
  529.8 553.0 %reduce-scatter.35.cloned.1.call-start = ((), (), s32[]{:S(2)}) async-start(), calls=%async_computation.30 | async-start | bytes 4456448 | tf_op jit(solution)/shard_map/reduce_scatter | solution.py:487
  541.3 621.3 %reduce-scatter.27.cloned.1.call-start = ((), (), s32[]{:S(2)}) async-start(), calls=%async_computation.26 | async-start | bytes 3899392 | tf_op jit(solution)/shard_map/reduce_scatter | solution.py:472
  546.1 38.3 %copy-start.56 = (f32[256,128]{0,1:T(8,128)S(1)}, f32[256,128]{0,1:T(8,128)}, u32[]{:S(2)}) copy-start(f32[256,128]{0,1:T(8,128)} %copy-done.55) | copy-start | bytes 393220
  606.3 3.2 collective-permute-start.2
  613.0 624.6 %reduce-scatter.37.cloned.1.call-start = ((), (), s32[]{:S(2)}) async-start(), calls=%async_computation.33 | async-start | bytes 278528
  631.9 680.8 %reduce-scatter.19.cloned.1.call-start = ((), (), s32[]{:S(2)}) async-start(), calls=%async_computation.22 | async-start | bytes 278528 | tf_op jit(solution)/shard_map/reduce_scatter | solution.py:460
  633.1 754.9 %reduce-scatter.21.cloned.1.call-start = ((), (), s32[]{:S(2)}) async-start(), calls=%async_computation.23 | async-start | bytes 278528 | tf_op jit(solution)/shard_map/reduce_scatter | solution.py:463
  634.8 820.6 %all-reduce.16.cloned.1.call-start = ((), (), s32[]{:S(2)}) async-start(), calls=%async_computation.34 | async-start | bytes 3080192 | tf_op jit(solution)/shard_map/psum | solution.py:492
  637.3 525.2 %copy-start.38 = (f32[259,1792]{1,0:T(8,128)S(1)}, f32[259,1792]{1,0:T(8,128)}, u32[]{:S(2)}) copy-start(f32[259,1792]{1,0:T(8,128)} %copy-done.37) | copy-start | bytes 5569540
  1162.6 70.4 %copy-start.120 = (f32[256]{0:T(256)S(1)}, f32[256]{0:T(256)}, u32[]{:S(2)}) copy-start(f32[256]{0:T(256)} %copy-done.119) | copy-start | bytes 3076
  1162.6 70.4 %copy-start.2 = (f32[256,1024]{1,0:T(8,128)S(1)}, f32[256,1024]{1,0:T(8,128)}, u32[]{:S(2)}) copy-start(f32[256,1024]{1,0:T(8,128)} %copy-done.1) | copy-start | bytes 3145732
  (118 other events, 687.9 us)
Sparse Core Ops, SparseCore 0:
  10.2 52.0 all-gather.19
  64.4 42.1 all-gather.15
  108.9 26.9 all-gather.31
  137.9 47.6 all-gather.21
  187.6 46.7 all-gather.23
  236.5 41.5 all-gather.17
  280.2 50.6 all-gather.25
  333.0 51.1 all-gather.27
  386.3 51.1 all-gather.29
  459.9 27.6 all-gather.33
  503.9 31.6 reduce-scatter.14
  538.6 71.5 reduce-scatter.16
  613.7 72.1 reduce-scatter.22
  689.1 74.9 reduce-scatter.24
  767.3 74.9 reduce-scatter.28
  845.5 76.8 reduce-scatter.30
  925.9 76.8 reduce-scatter.32
  1005.9 76.8 reduce-scatter.34
  1086.6 75.9 reduce-scatter.26
  1166.4 71.1 reduce-scatter.36
  1241.4 71.2 reduce-scatter.18
  1316.8 71.2 reduce-scatter.20
  1391.1 64.2 all-reduce.15
where the time goes:
time: 1480 us; the launch traced here: 1470 us
  waiting for transfers between devices  917 us (62%)
  blocking collectives  208 us (14%)
  matrix products  163 us (11%)
  other arithmetic  102 us (7%)
  local copies, waits for them, and re-layouts  60 us (4%)
  between operations  17.5 us (1%)
    reduce_scatter x1, waiting for transfers between devices, on_device(): lax.psum_scatter(grad_feed_up.astype(jnp.bfloat16), 'dp', scatter_dimensi...  80.4 us
    reduce_scatter x1, waiting for transfers between devices, on_device(): lax.psum_scatter(grad_feed_down.astype(jnp.bfloat16), 'dp', scatter_dimen...  80.1 us
    reduce_scatter x1, waiting for transfers between devices, on_device(): lax.psum_scatter(grad_feed_gate.astype(jnp.bfloat16), 'dp', scatter_dimen...  80.1 us
    reduce_scatter x1, waiting for transfers between devices, on_device(): lax.psum_scatter(grad_mixer_weight.astype(jnp.bfloat16), 'dp', scatter_di...  79.7 us
    reduce_scatter x1, waiting for transfers between devices, on_device(): lax.psum_scatter(grad_gate_weight.astype(jnp.bfloat16), 'dp', scatter_dim...  78.2 us
    reduce_scatter x1, waiting for transfers between devices, on_device(): lax.psum_scatter(grad_mixer_out.astype(jnp.bfloat16), 'dp', scatter_dimen...  78.2 us
    reduce_scatter x1, waiting for transfers between devices, on_device(): lax.psum_scatter(grad_value_weight.astype(jnp.bfloat16), 'dp', scatter_di...  75.4 us
    reduce_scatter x1, waiting for transfers between devices, on_device(): lax.psum_scatter(grad_key_weight.astype(jnp.bfloat16), 'dp', scatter_dime...  74.3 us
  transfers between devices with their start and end apart: 26, of which 18 were waited for; matrix products, arithmetic and copies ran while one was open for 19% of the time, Pallas kernels for 0%

commit v1 on v0

--- a/solution.py
+++ b/solution.py
@@ -18,6 +18,10 @@
 attention_multiplier = 0.9375
 mixer_multiplier = 0.2357
 rotary_base = 100000000000.0
+IN_USED = 4120
+IN_WIDTH = 4352
+CHIP_GROUPS = [[2 * z + c for z in range(4)] for c in range(2)]
+CORE_GROUPS = [[8 * d + 2 * z + c for d in range(16) for z in range(4)] for c in range(2)]
 
 
 def from_behind(block, axis, distance):
@@ -26,28 +30,87 @@
     return lax.ppermute(block, axis, route)
 
 
-def carried_in(shard, axis, combine, identity, reverse):
-    length, mine = (lax.axis_size(axis), lax.axis_index(axis))
-    everything = jax.tree.map(
-        lambda part, kind: lax.all_gather(part.astype(kind), axis),
-        shard,
-        (jnp.bfloat16, jnp.bfloat16),
-    )
-    start = jax.tree.map(
-        lambda part, zero: jnp.broadcast_to(jnp.asarray(zero, part.dtype), part.shape),
-        shard,
-        identity,
-    )
-
-    def turn(k, before):
-        at = length - 1 - k if reverse else k
-        reached = at > mine if reverse else at < mine
-        new = combine(
-            before, jax.tree.map(lambda part, own: part[at].astype(own.dtype), everything, shard)
-        )
-        return jax.tree.map(lambda a, b: jnp.where(reached, a, b), new, before)
-
-    return lax.fori_loop(0, length, turn, start)
+def swap_cores(block):
+    devices = range(lax.axis_size("context"))
+    return lax.ppermute(block, "context", [(i, i ^ 1) for i in devices])
+
+
+def shift_chips(block, distance):
+    devices = lax.axis_size("context")
+    return lax.ppermute(
+        block, "context", [(i, (i + 2 * distance) % devices) for i in range(devices)]
+    )
+
+
+def shift_rows(block, distance, stride):
+    route = []
+    for i in range(16):
+        place = i // stride % 4
+        route.append((i, i + ((place + distance) % 4 - place) * stride))
+    return lax.ppermute(block, "dp", route)
+
+
+def sum_of_four(block, shift):
+    one, two, three = shift(block, 1), shift(block, 2), shift(block, 3)
+    return (block + two) + (one + three)
+
+
+def sum_everywhere(block):
+    block = block + swap_cores(block)
+    block = sum_of_four(block, shift_chips)
+    block = sum_of_four(block, lambda part, k: shift_rows(part, k, 1))
+    return sum_of_four(block, lambda part, k: shift_rows(part, k, 4))
+
+
+def half(block, which, axis):
+    size = block.shape[axis] // 2
+    return lax.dynamic_slice_in_dim(block, which * size, size, axis)
+
+
+def copies_of(block):
+    devices = lax.axis_size("context")
+    return lax.all_to_all(
+        jnp.broadcast_to(block[None], (devices,) + block.shape), "context", 0, 0
+    )
+
+
+def carried_in(carried, local, reverse):
+    mine = lax.axis_index("context")
+    core, chip = mine % 2, mine // 2
+    is_first = (core == 1) if reverse else (core == 0)
+    order = 3 - chip if reverse else chip
+    way = -1 if reverse else 1
+    decay_other = swap_cores(carried)
+    own_part, own_decay = half(local, core, 0), half(carried, core, 0)
+    got_part = swap_cores(half(local, 1 - core, 0).astype(jnp.bfloat16)).astype(jnp.float32)
+    got_decay = half(decay_other, core, 0)
+    first = jnp.where(is_first, own_part, got_part)
+    second = jnp.where(is_first, got_part, own_part)
+    first_decay = jnp.where(is_first, own_decay, got_decay)
+    second_decay = jnp.where(is_first, got_decay, own_decay)
+    if reverse:
+        chip_part = first * second_decay[:, None, None] + second
+    else:
+        chip_part = first * second_decay[:, None, None] + second
+    chip_low = chip_part.astype(jnp.bfloat16)
+    chip_decay = first_decay * second_decay
+    total = jnp.zeros_like(first)
+    factor = jnp.ones_like(chip_decay)
+    for k in range(1, 4):
+        part = shift_chips(chip_low, way * k).astype(jnp.float32)
+        reach = jnp.where(order >= k, factor, 0.0)
+        total = total + reach[:, None, None] * part
+        if k < 3:
+            factor = factor * shift_chips(chip_decay, way * k)
+    for_first = total
+    for_second = total * first_decay[:, None, None] + first
+    keep = jnp.where(is_first, for_first, for_second)
+    give = jnp.where(is_first, for_second, for_first)
+    got = swap_cores(give.astype(jnp.bfloat16))
+    keep = keep.astype(jnp.bfloat16)
+    return jnp.where(
+        core == 0, jnp.concatenate([keep, got], axis=0), jnp.concatenate([got, keep], axis=0)
+    )
 
 
 def rms_norm(values, gain_vector):
@@ -113,7 +176,7 @@
     return (within, entry, leaving, carried)
 
 
-def attention_scores(rotated_queries, every_key, query_places, seg_own, seg_all):
+def attention_scores(rotated_queries, every_key, query_places, key_places, seg_own, seg_all):
     count_of_rows = rotated_queries.shape[0]
     count_of_keys = every_key.shape[0]
     heads_of_queries = rotated_queries.reshape(
@@ -123,7 +186,7 @@
     raw_scores = jnp.einsum(
         "rgqd,lgd->gqrl", heads_of_queries, heads_of_keys, preferred_element_type=jnp.float32
     ) * (1.0 / math.sqrt(HEAD_WIDTH))
-    allowed = (jnp.arange(count_of_keys)[None, :] <= query_places[:, None]) & (
+    allowed = (key_places[None, :] <= query_places[:, None]) & (
         seg_all[None, :] == seg_own[:, None]
     )
     return jnp.where(allowed[None, None], raw_scores, masked_fill)
@@ -180,37 +243,36 @@
     feed_up,
     feed_down,
 ):
-    gathered = (
-        lax.all_gather(query_weight, "dp", axis=0, tiled=True),
-        lax.all_gather(key_matrix, "dp", axis=0, tiled=True),
-        lax.all_gather(value_matrix, "dp", axis=0, tiled=True),
-        lax.all_gather(attention_out, "dp", axis=0, tiled=True),
-        lax.all_gather(gate_weight, "dp", axis=0, tiled=True),
-        lax.all_gather(mixer_weight, "dp", axis=0, tiled=True),
-        lax.all_gather(step_weight, "dp", axis=0, tiled=True),
-        lax.all_gather(mixer_out, "dp", axis=0, tiled=True),
-        lax.all_gather(feed_gate, "dp", axis=0, tiled=True),
-        lax.all_gather(feed_up, "dp", axis=0, tiled=True),
-        lax.all_gather(feed_down, "dp", axis=0, tiled=True),
-    )
-    (
-        query_full,
-        key_full,
-        value_full,
-        out_full,
-        gate_full,
-        mixer_full,
-        step_full,
-        mixer_out_full,
-        ffn_gate_full,
-        ffn_up_full,
-        ffn_down_full,
-    ) = gathered
+    block_index = lax.axis_index("context")
+    core = block_index % 2
+    chip = block_index // 2
+    both = ("dp", "context")
+    step_padded = jnp.pad(step_weight, ((0, 0), (0, IN_WIDTH - IN_USED)))
+    in_shard = jnp.concatenate(
+        [query_weight, key_matrix, value_matrix, gate_weight, mixer_weight, step_padded], axis=1
+    )
+    in_full = lax.all_gather(
+        lax.dynamic_slice_in_dim(in_shard, block_index * 8, 8, 0), both, axis=0, tiled=True
+    )
+    feed_shard = lax.dynamic_slice_in_dim(
+        jnp.concatenate([feed_gate, feed_up], axis=1), block_index * 8, 8, 0
+    )
+    out_shard = lax.dynamic_slice_in_dim(
+        jnp.concatenate([attention_out, mixer_out, feed_down], axis=0), block_index * 32, 32, 0
+    )
+    out_shard = out_shard.reshape(4, 8, 1024).transpose(1, 0, 2).reshape(8, 4096)
+    late_full = lax.all_gather(
+        jnp.concatenate([feed_shard, out_shard], axis=1), both, axis=0, tiled=True
+    )
+    feed_full = late_full[:, :4096]
+    out_parts = late_full[:, 4096:].reshape(16, 8, 8, 4, 1024).transpose(0, 1, 3, 2, 4)
+    out_full = out_parts[:, 0].reshape(512, 1024)
+    mixer_out_full = out_parts[:, 1:4].reshape(1536, 1024)
+    ffn_down_full = out_parts[:, 4:].reshape(2048, 1024)
     count_of_rows = tokens.shape[0]
     tap_count = conv_weight.shape[0]
     inner_width = MH * MP
     width_of_keys = KEY_VALUE_HEADS * HEAD_WIDTH
-    block_index = lax.axis_index("context")
     query_places = block_index * count_of_rows + jnp.arange(count_of_rows, dtype=jnp.int32)
     place_float = query_places.astype(jnp.float32)
     seg_float = segments.astype(jnp.float32)
@@ -218,23 +280,42 @@
     hidden_in = tokens.astype(jnp.float32)
     normed, norm_one_back = jax.vjp(rms_norm, hidden_in, attention_gain)
     normed_low = normed.astype(jnp.bfloat16)
-    query_lin = project(normed_low, query_full)
-    key_lin = project(normed_low, key_full)
-    value_lin = project(normed_low, value_full)
+    every_lin = project(normed_low, in_full)
+    query_lin = every_lin[:, :512]
+    key_lin = every_lin[:, 512:640]
+    value_lin = every_lin[:, 640:768]
+    gate_lin = every_lin[:, 768:2304]
+    mixer_lin = every_lin[:, 2304:4096]
+    step_lin = every_lin[:, 4096:IN_USED]
     rotated_queries = rotary(query_lin, place_float, 1.0).astype(jnp.bfloat16)
     rotated_keys = rotary(key_lin, place_float, 1.0).astype(jnp.bfloat16)
     value_reduced = value_lin.astype(jnp.bfloat16)
-    every_key, every_value, seg_all = (
-        lax.all_gather(rotated_keys, "context", axis=0, tiled=True),
-        lax.all_gather(value_reduced, "context", axis=0, tiled=True),
-        lax.all_gather(seg_low, "context", axis=0, tiled=True),
-    )
+    sent = jnp.concatenate(
+        [
+            jnp.concatenate([rotated_keys, value_reduced], axis=1),
+            jnp.pad(seg_low[None, :], ((0, 7), (0, 0))),
+        ],
+        axis=0,
+    )
+    along = jnp.stack([sent] + [shift_chips(sent, k) for k in range(1, 4)])
+    slots = jnp.concatenate([along, swap_cores(along)], axis=0)
+    every_key = slots[:, :count_of_rows, :width_of_keys].reshape(-1, width_of_keys)
+    every_value = slots[:, :count_of_rows, width_of_keys:].reshape(-1, width_of_keys)
+    seg_all = slots[:, count_of_rows].reshape(-1)
+    owners = jnp.concatenate(
+        [(chip - jnp.arange(4)) % 4 * 2 + core, (chip - jnp.arange(4)) % 4 * 2 + 1 - core]
+    )
+    key_places = (
+        owners[:, None] * count_of_rows + jnp.arange(count_of_rows, dtype=jnp.int32)[None, :]
+    ).reshape(-1)
     heads_of_keys = every_key.reshape(-1, KEY_VALUE_HEADS, HEAD_WIDTH)
     heads_of_values = every_value.reshape(-1, KEY_VALUE_HEADS, HEAD_WIDTH)
     heads_of_queries = rotated_queries.reshape(
         count_of_rows, KEY_VALUE_HEADS, QUERY_HEADS // KEY_VALUE_HEADS, HEAD_WIDTH
     )
-    scores = attention_scores(rotated_queries, every_key, query_places, seg_low, seg_all)
+    scores = attention_scores(
+        rotated_queries, every_key, query_places, key_places, seg_low, seg_all
+    )
     top_score = jnp.max(scores, axis=-1, keepdims=True)
     exponent = jnp.exp(scores - top_score)
     totals = jnp.sum(exponent, axis=-1, keepdims=True)
@@ -245,9 +326,6 @@
     )
     attended_low = attended.reshape(count_of_rows, QUERY_HEADS * HEAD_WIDTH).astype(jnp.bfloat16)
     attention_branch = project(attended_low, out_full)
-    gate_lin = project(normed_low, gate_full)
-    mixer_lin = project(normed_low, mixer_full)
-    step_lin = project(normed_low, step_full)
     prev_rows, prev_segs = from_behind(
         (mixer_lin[count_of_rows - tap_count + 1 :], seg_float[count_of_rows - tap_count + 1 :]),
         "context",
@@ -288,11 +366,7 @@
     local_state = jnp.einsum(
         "jhn,jhp->hnp", weighted_low, inputs_low, preferred_element_type=jnp.float32
     )
-    identity = (jnp.ones((MH,), jnp.float32), jnp.zeros((MH, NS, MP), jnp.float32))
-    incoming_decay, incoming = carried_in(
-        (carried, local_state), "context", chain_forward, identity, False
-    )
-    incoming_low = incoming.astype(jnp.bfloat16)
+    incoming_low = carried_in(carried, local_state, False)
     from_state = jnp.einsum("in,hnp->ihp", seas, incoming_low, preferred_element_type=jnp.float32)
     scanned = inner + from_state * entry[:, :, None] + skip_gain[None, :, None] * mixer_x
     gated, gating_back = jax.vjp(gating, scanned.reshape(count_of_rows, inner_width), gate_lin)
@@ -301,58 +375,57 @@
     residual = hidden_in + attention_multiplier * attention_branch + mixer_multiplier * mixer_branch
     normed_two, norm_two_back = jax.vjp(rms_norm, residual, feed_gain)
     normed_two_low = normed_two.astype(jnp.bfloat16)
-    ffn_gate_lin = project(normed_two_low, ffn_gate_full)
-    ffn_up_lin = project(normed_two_low, ffn_up_full)
+    feed_lin = project(normed_two_low, feed_full)
+    ffn_gate_lin = feed_lin[:, :2048]
+    ffn_up_lin = feed_lin[:, 2048:]
     hidden_act, swiglu_back = jax.vjp(swiglu, ffn_gate_lin, ffn_up_lin)
     hidden_low = hidden_act.astype(jnp.bfloat16)
     output = (residual + project(hidden_low, ffn_down_full)).astype(jnp.bfloat16)
-    again = (
-        lax.all_gather(query_weight, "dp", axis=0, tiled=True),
-        lax.all_gather(key_matrix, "dp", axis=0, tiled=True),
-        lax.all_gather(value_matrix, "dp", axis=0, tiled=True),
-        lax.all_gather(attention_out, "dp", axis=0, tiled=True),
-        lax.all_gather(gate_weight, "dp", axis=0, tiled=True),
-        lax.all_gather(mixer_weight, "dp", axis=0, tiled=True),
-        lax.all_gather(step_weight, "dp", axis=0, tiled=True),
-        lax.all_gather(mixer_out, "dp", axis=0, tiled=True),
-        lax.all_gather(feed_gate, "dp", axis=0, tiled=True),
-        lax.all_gather(feed_up, "dp", axis=0, tiled=True),
-        lax.all_gather(feed_down, "dp", axis=0, tiled=True),
-    )
-    (
-        query_back,
-        key_back,
-        value_back,
-        out_back,
-        gate_back,
-        mixer_in_back,
-        step_back,
-        mixer_out_back,
-        ffn_gate_back,
-        ffn_up_back,
-        ffn_down_back,
-    ) = again
     upstream = cotangent.astype(jnp.float32)
-    grad_feed_down = input_grad(hidden_low, cotangent)
-    d_hidden = back_through(cotangent, ffn_down_back)
+    d_hidden = back_through(cotangent, ffn_down_full)
     d_ffn_gate, d_ffn_up = swiglu_back(d_hidden)
-    d_ffn_gate_low = d_ffn_gate.astype(jnp.bfloat16)
-    d_ffn_up_low = d_ffn_up.astype(jnp.bfloat16)
-    grad_feed_gate = input_grad(normed_two_low, d_ffn_gate_low)
-    grad_feed_up = input_grad(normed_two_low, d_ffn_up_low)
-    d_normed_two = back_through(d_ffn_gate_low, ffn_gate_back) + back_through(
-        d_ffn_up_low, ffn_up_back
-    )
+    d_feed_low = jnp.concatenate([d_ffn_gate, d_ffn_up], axis=1).astype(jnp.bfloat16)
+    d_normed_two = back_through(d_feed_low, feed_full)
     d_resid_norm, grad_feed_gain = norm_two_back(d_normed_two)
     d_residual = upstream + d_resid_norm
     d_attn_low = (attention_multiplier * d_residual).astype(jnp.bfloat16)
     d_mixer_low = (mixer_multiplier * d_residual).astype(jnp.bfloat16)
-    grad_attention_out = input_grad(attended_low, d_attn_low)
-    grad_mixer_out = input_grad(gated_low, d_mixer_low)
-    attended_gradient = back_through(d_attn_low, out_back).astype(jnp.bfloat16)
-    d_gated = back_through(d_mixer_low, mixer_out_back)
+
+    def early_grads(which):
+        feed = input_grad(normed_two_low, half(d_feed_low, which, 1)).astype(jnp.bfloat16)
+        attn = input_grad(attended_low, half(d_attn_low, which, 1)).astype(jnp.bfloat16)
+        mix = input_grad(gated_low, half(d_mixer_low, which, 1)).astype(jnp.bfloat16)
+        down = input_grad(hidden_low, half(cotangent, which, 1)).astype(jnp.bfloat16)
+        return (feed, attn, mix, down)
+
+    early_got = jax.tree.map(swap_cores, early_grads(1 - core))
+    early = jax.tree.map(lambda a, b: a + b, early_grads(core), early_got)
+    early_rows = jnp.concatenate(
+        [
+            early[1].reshape(16, 32, 512),
+            early[2].reshape(16, 96, 512),
+            early[3].reshape(16, 128, 512),
+            early[0].reshape(16, 64, 4, 512).transpose(0, 2, 1, 3).reshape(16, 256, 512),
+        ],
+        axis=1,
+    )
+    early_shard = lax.psum_scatter(
+        early_rows.reshape(16 * 512, 512), "dp", scatter_dimension=0, tiled=True
+    )
+    early_parts = lax.all_to_all(
+        early_shard.reshape(4, 128, 512), "context", 0, 0, axis_index_groups=CHIP_GROUPS
+    )
+    early_sum = jnp.sum(early_parts.astype(jnp.float32), axis=0).astype(jnp.bfloat16)
+    early_all = copies_of(early_sum).reshape(4, 2, 128, 512).astype(jnp.float32)
+    early_out = early_all[:2].transpose(0, 2, 1, 3).reshape(256, 1024)
+    early_feed = early_all[2:].transpose(1, 0, 2, 3).reshape(2, 4, 64, 512)
+    early_feed = early_feed.transpose(0, 2, 1, 3).reshape(2, 64, 2048)
+    attended_gradient = back_through(d_attn_low, out_full).astype(jnp.bfloat16)
+    d_gated = back_through(d_mixer_low, mixer_out_full)
     scale_factor = 1.0 / math.sqrt(HEAD_WIDTH)
-    scores_again = attention_scores(rotated_queries, every_key, query_places, seg_low, seg_all)
+    scores_again = attention_scores(
+        rotated_queries, every_key, query_places, key_places, seg_low, seg_all
+    )
     probs_again = jnp.exp(scores_again - log_total)
     probs_again_low = probs_again.astype(jnp.bfloat16)
     output_heads_gradient = attended_gradient.reshape(
@@ -378,12 +451,13 @@
     d_values = jnp.einsum(
         "gqrl,rgqd->lgd", probs_again_low, output_heads_gradient, preferred_element_type=jnp.float32
     ).reshape(count_of_rows * lax.axis_size("context"), width_of_keys)
-    key_grads = lax.psum_scatter(
-        jnp.concatenate([d_keys, d_values], axis=1).astype(jnp.bfloat16),
-        "context",
-        scatter_dimension=0,
-        tiled=True,
-    ).astype(jnp.float32)
+    slot_grads = jnp.concatenate([d_keys, d_values], axis=1).astype(jnp.bfloat16)
+    slot_grads = slot_grads.reshape(2, 4, count_of_rows, 2 * width_of_keys)
+    chip_grads = slot_grads[0].astype(jnp.float32) + swap_cores(slot_grads[1]).astype(jnp.float32)
+    chip_low = chip_grads.astype(jnp.bfloat16)
+    key_grads = chip_grads[0]
+    for k in range(1, 4):
+        key_grads = key_grads + shift_chips(chip_low[k], -k).astype(jnp.float32)
     d_query_low = rotary(d_query_rot, place_float, -1.0).astype(jnp.bfloat16)
     d_key_low = rotary(key_grads[:, :width_of_keys], place_float, -1.0).astype(jnp.bfloat16)
     d_value_low = key_grads[:, width_of_keys:].astype(jnp.bfloat16)
@@ -408,11 +482,10 @@
         "ij,jn->in", d_intersection_low, bees, preferred_element_type=jnp.float32
     )
     d_bees = jnp.einsum("ij,in->jn", d_intersection_low, seas, preferred_element_type=jnp.float32)
-    outgoing_decay, d_outgoing = carried_in(
-        (carried, d_incoming), "context", chain_backward, identity, True
-    )
-    d_state_low = d_outgoing.astype(jnp.bfloat16)
-    d_carried = jnp.sum(d_outgoing * incoming, axis=(1, 2))
+    d_state_low = carried_in(carried, d_incoming, True)
+    d_carried = jnp.sum(
+        d_state_low.astype(jnp.float32) * incoming_low.astype(jnp.float32), axis=(1, 2)
+    )
     d_weighted = jnp.einsum(
         "jhp,hnp->jhn", inputs_low, d_state_low, preferred_element_type=jnp.float32
     )
@@ -434,84 +507,66 @@
     d_mixer_lin = d_extended[tap_count - 1 :] + jnp.pad(
         rim_back, ((count_of_rows - tap_count + 1, 0), (0, 0))
     )
-    d_gate_low = d_gate_lin.astype(jnp.bfloat16)
-    d_mixer_in_low = d_mixer_lin.astype(jnp.bfloat16)
-    d_step_low = d_step_lin.astype(jnp.bfloat16)
-    grad_query_weight = input_grad(normed_low, d_query_low)
-    grad_key_weight = input_grad(normed_low, d_key_low)
-    grad_value_weight = input_grad(normed_low, d_value_low)
-    grad_gate_weight = input_grad(normed_low, d_gate_low)
-    grad_mixer_weight = input_grad(normed_low, d_mixer_in_low)
-    grad_step_weight = input_grad(normed_low, d_step_low)
-    d_normed = (
-        back_through(d_query_low, query_back)
-        + back_through(d_key_low, key_back)
-        + back_through(d_value_low, value_back)
-        + back_through(d_gate_low, gate_back)
-        + back_through(d_mixer_in_low, mixer_in_back)
-        + back_through(d_step_low, step_back)
-    )
+    d_every_low = jnp.concatenate(
+        [
+            d_query_low,
+            d_key_low,
+            d_value_low,
+            d_gate_lin.astype(jnp.bfloat16),
+            d_mixer_lin.astype(jnp.bfloat16),
+            jnp.pad(d_step_lin, ((0, 0), (0, IN_WIDTH - IN_USED))).astype(jnp.bfloat16),
+        ],
+        axis=1,
+    )
+    late_got = swap_cores(
+        input_grad(normed_low, half(d_every_low, 1 - core, 1)).astype(jnp.bfloat16)
+    )
+    late = input_grad(normed_low, half(d_every_low, core, 1)) + late_got.astype(jnp.float32)
+    late_parts = lax.all_to_all(
+        late.astype(jnp.bfloat16).reshape(64, 16, IN_WIDTH // 2),
+        both,
+        0,
+        0,
+        axis_index_groups=CORE_GROUPS,
+    )
+    late_sum = jnp.sum(late_parts.astype(jnp.float32), axis=0).astype(jnp.bfloat16)
+    late_all = copies_of(late_sum).reshape(4, 2, 16, IN_WIDTH // 2).astype(jnp.float32)
+    late_all = late_all.transpose(0, 2, 1, 3).reshape(64, IN_WIDTH)
+    d_normed = back_through(d_every_low, in_full)
     d_tokens_norm, grad_attention_gain = norm_one_back(d_normed)
     grad_tokens = d_residual + d_tokens_norm
+
+    def flat(part):
+        part = part.reshape(-1)
+        return jnp.pad(part, (0, -part.size % 128))
+
     pieces = (
-        lax.psum_scatter(
-            grad_query_weight.astype(jnp.bfloat16), "dp", scatter_dimension=0, tiled=True
-        ).astype(jnp.float32),
-        lax.psum_scatter(
-            grad_key_weight.astype(jnp.bfloat16), "dp", scatter_dimension=0, tiled=True
-        ).astype(jnp.float32),
-        lax.psum_scatter(
-            grad_value_weight.astype(jnp.bfloat16), "dp", scatter_dimension=0, tiled=True
-        ).astype(jnp.float32),
-        lax.psum_scatter(
-            grad_attention_out.astype(jnp.bfloat16), "dp", scatter_dimension=0, tiled=True
-        ).astype(jnp.float32),
-        lax.psum_scatter(
-            grad_gate_weight.astype(jnp.bfloat16), "dp", scatter_dimension=0, tiled=True
-        ).astype(jnp.float32),
-        lax.psum_scatter(
-            grad_mixer_weight.astype(jnp.bfloat16), "dp", scatter_dimension=0, tiled=True
-        ).astype(jnp.float32),
-        lax.psum_scatter(
-            grad_step_weight.astype(jnp.bfloat16), "dp", scatter_dimension=0, tiled=True
-        ).astype(jnp.float32),
-        lax.psum_scatter(
-            grad_mixer_out.astype(jnp.bfloat16), "dp", scatter_dimension=0, tiled=True
-        ).astype(jnp.float32),
-        lax.psum_scatter(
-            grad_feed_gate.astype(jnp.bfloat16), "dp", scatter_dimension=0, tiled=True
-        ).astype(jnp.float32),
-        lax.psum_scatter(
-            grad_feed_up.astype(jnp.bfloat16), "dp", scatter_dimension=0, tiled=True
-        ).astype(jnp.float32),
-        lax.psum_scatter(
-            grad_feed_down.astype(jnp.bfloat16), "dp", scatter_dimension=0, tiled=True
-        ).astype(jnp.float32),
-    )
+        grad_attention_gain,
+        grad_conv_weight,
+        grad_conv_bias,
+        grad_step_bias,
+        grad_decay_log,
+        grad_skip_gain,
+        grad_feed_gain,
+    )
+    packed = jnp.concatenate([flat(part) for part in pieces])
+    packed = sum_everywhere(jnp.pad(packed, (0, -packed.size % 1024)).reshape(-1, 128)).reshape(-1)
+    small, start = [], 0
+    for part in pieces:
+        small.append(packed[start : start + part.size].reshape(part.shape))
+        start += part.size + -part.size % 128
     summed = (
-        lax.psum(pieces[0].astype(jnp.bfloat16), "context").astype(jnp.float32),
-        lax.psum(pieces[1].astype(jnp.bfloat16), "context").astype(jnp.float32),
-        lax.psum(pieces[2].astype(jnp.bfloat16), "context").astype(jnp.float32),
-        lax.psum(pieces[3].astype(jnp.bfloat16), "context").astype(jnp.float32),
-        lax.psum(pieces[4].astype(jnp.bfloat16), "context").astype(jnp.float32),
-        lax.psum(pieces[5].astype(jnp.bfloat16), "context").astype(jnp.float32),
-        lax.psum(pieces[6].astype(jnp.bfloat16), "context").astype(jnp.float32),
-        lax.psum(pieces[7].astype(jnp.bfloat16), "context").astype(jnp.float32),
-        lax.psum(pieces[8].astype(jnp.bfloat16), "context").astype(jnp.float32),
-        lax.psum(pieces[9].astype(jnp.bfloat16), "context").astype(jnp.float32),
-        lax.psum(pieces[10].astype(jnp.bfloat16), "context").astype(jnp.float32),
-    )
-    small = lax.psum(
-        (
-            grad_attention_gain,
-            grad_conv_weight,
-            grad_conv_bias,
-            grad_step_bias,
-            grad_decay_log,
-            grad_skip_gain,
-            grad_feed_gain,
-        ),
-        ("dp", "context"),
+        late_all[:, :512],
+        late_all[:, 512:640],
+        late_all[:, 640:768],
+        early_out[:32],
+        late_all[:, 768:2304],
+        late_all[:, 2304:4096],
+        late_all[:, 4096:IN_USED],
+        early_out[32:128],
+        early_feed[0],
+        early_feed[1],
+        early_out[128:],
     )
     return (
         output,

time: 1480 us -> 622 us (0.42)
  waiting for transfers between devices: 917 us -> 178 us
  blocking collectives: 208 us -> 0 us
  local copies, waits for them, and re-layouts: 60 us -> 120 us
  starting transfers between devices: 5.62 us -> 65.4 us
  other arithmetic: 102 us -> 78.9 us
    reduce_scatter x11 -> x1, waiting for transfers between devices: 673 us -> 0.01 us  [on_device(): lax.psum_scatter(early_rows.reshape(16 * 512, 512), 'dp', scatter_dimensi...]
    all_gather x10 -> x2, waiting for transfers between devices: 195 us -> 61.5 us  [the longest x1 61.5 us: on_device(): lax.all_gather(lax.dynamic_slice_in_dim(in_shard, block_index * 8, 8, 0),...]
    all_gather x7 -> x0, blocking collectives: 118 us -> none  [the longest x1 24.5 us: on_device(): lax.all_gather(step_weight, 'dp', axis=0, tiled=True)]
    ppermute x0 -> x38, waiting for transfers between devices: none -> 93 us  [the longest x19 79.7 us: shift_chips(): lax.ppermute(block, 'context', [(i, (i + 2 * distance) % devices) for i i...]
    psum x2 -> x0, blocking collectives: 90 us -> none  [the longest x1 65.4 us: on_device(): lax.psum((grad_attention_gain, grad_conv_weight, grad_conv_bias, grad_ste...]
    ppermute x0 -> x38, starting transfers between devices: none -> 41.1 us  [the longest x19 24.2 us: shift_chips(): lax.ppermute(block, 'context', [(i, (i + 2 * distance) % devices) for i i...]
    psum x1 -> x0, waiting for transfers between devices: 40.8 us -> none  [on_device(): lax.psum(pieces[0].astype(jnp.bfloat16), 'context').astype(jnp.float32)]
    slice x3 -> x36, local copies, waits for them, and re-layouts: 0.93 us -> 31.3 us  [the longest x1 7.82 us: on_device(): late_full[:, 4096:].reshape(16, 8, 8, 4, 1024).transpose(0, 1, 3, 2, 4)]
  transfers between devices with their start and end apart: 26 -> 48, of which waited for: 18 -> 22; matrix products, arithmetic and copies ran while one was open for 19% -> 39% of each run, Pallas kernels for 0% -> 0%
where the time goes in v1:
time: 622 us; the launch traced here: 610 us
  waiting for transfers between devices  178 us (29%)
  matrix products  150 us (24%)
  local copies, waits for them, and re-layouts  120 us (19%)
  other arithmetic  78.9 us (13%)
  starting transfers between devices  65.4 us (11%)
  between operations  17.5 us (3%)
    ppermute x19, waiting for transfers between devices, shift_chips(): lax.ppermute(block, 'context', [(i, (i + 2 * distance) % devices) for i i...  79.7 us
    all_gather x1, waiting for transfers between devices, on_device(): lax.all_gather(lax.dynamic_slice_in_dim(in_shard, block_index * 8, 8, 0),...  61.5 us
    dot_general x10, matrix products, input_grad(): jnp.einsum('rk,rj->kj', left, right, preferred_element_type=jnp.float32)  36.8 us
    unnamed x310, local copies, waits for them, and re-layouts  32.7 us
    ppermute x19, starting transfers between devices, shift_chips(): lax.ppermute(block, 'context', [(i, (i + 2 * distance) % devices) for i i...  24.2 us
    dot_general x5, matrix products, back_through(): jnp.einsum('rj,kj->rk', grad_low, weight_full, preferred_element_type=jnp...  23.9 us
    all_to_all x2, waiting for transfers between devices, copies_of(): lax.all_to_all(jnp.broadcast_to(block[None], (devices,) + block.shape), '...  19.8 us
    dot_general x5, matrix products, project(): return jnp.dot(left, right, preferred_element_type=jnp.float32)  14 us
  transfers between devices with their start and end apart: 48, of which 22 were waited for; matrix products, arithmetic and copies ran while one was open for 39% of the time, Pallas kernels for 0%

profile of v1, /device:TPU:0, one launch (start us, length us, event | category | flops | bytes accessed | tf_op | source)
XLA Modules:
  0.0 609.6 jit_solution(6424518898108394010)
XLA Ops:
  24.6 61.5 %all-gather.3.cloned.1.call-done = bf16[1024,4352]{1,0:T(8,128)(2,1)} async-done(((bf16[8,4352]{1,0:T(8,128)(2,1)}), bf16[1024,4352]{1,0:T(8,128)(2,1)}) %all-gather.3.cloned.1.call-update) | async-done | bytes 8912912 | tf_op jit(solution)/shard_map/all_gather | solution.py:254
  86.1 6.1 fusion.167
  119.7 3.8 collective-permute-done.9
  124.6 4.0 collective-permute-done.22
  128.6 3.5 collective-permute-done.20
  132.7 4.2 fusion.176
  140.0 3.6 copy.221
  153.9 8.3 %collective-permute-done.12 = bf16[12,128,64]{1,2,0:T(8,128)(2,1)S(1)} collective-permute-done((bf16[12,128,64]{1,2,0:T(8,128)(2,1)S(1)}, bf16[12,128,64]{1,2,0:T(8,128)(2,1)S(1)}, u32[]{:S(2)}, u32[]{:S(2)}) %collective-permute-start.12) | collective-permute-done | bytes 196640 | tf_op jit(solution)/shard_map/ppermute | solution.py:40
  164.5 4.7 collective-permute-done.8
  192.3 8.2 %fusion.184 = (f32[2,4,256]{2,1,0:T(4,128)S(1)}, f32[2,4,256,2048]{2,3,1,0:T(8,128)}) fusion(bf16[256,2,4,64]{0,3,2,1:T(8,128)(2,1)} %bitcast.344, bf16[2048,2,64,1]{0,2,1,3:T(8,128)(2,1)S(1)} %reshape.599, pred[256,2048]{0,1:T(8,128)(4,1)S(1)} %compare_and_fusion), kind=kOutput, calls=%fused_computation.393 | convolution fusion | flops 549451776 | bytes 18096128 | tf_op jit(solution)/shard_map/rgqd,lgd->gqrl/dot_general | solution.py:186
  200.5 8.0 %fusion.3 = f32[2,4,256]{2,1,0:T(4,128)S(1)} fusion(f32[2,4,256,2048]{2,3,1,0:T(8,128)} %get-tuple-element.226, f32[2,4,256]{2,1,0:T(4,128)S(1)} %get-tuple-element.225), kind=kLoop, calls=%fused_computation.9 | loop fusion | flops 8386560 | bytes 16793600 | tf_op jit(solution)/shard_map/reduce_sum | solution.py:321
  208.5 8.2 %fusion.70 = bf16[2,64,4,256]{3,1,2,0:T(8,128)(2,1)} fusion(f32[2,4,256,2048]{2,3,1,0:T(8,128)} %get-tuple-element.226, f32[2,4,256]{2,1,0:T(4,128)S(1)} %fusion.3, f32[2,4,256]{2,1,0:T(4,128)S(1)} %get-tuple-element.225, bf16[2048,2,64,1]{0,2,1,3:T(8,128)(2,1)S(1)} %copy-done.44), kind=kOutput, calls=%fused_computation.142 | convolution fusion | flops 549584896 | bytes 17580032 | tf_op jit(solution)/shard_map/gqrl,lgd->rgqd/dot_general | solution.py:324
  216.8 7.8 %slice.350 = bf16[1024,4096]{1,0:T(8,128)(2,1)} slice(bf16[1024,8192]{1,0:T(8,128)(2,1)} %all-gather.5.cloned.1.call-done), slice={[0:1024], [4096:8192]} | slice | bytes 16777216 | tf_op jit(solution)/shard_map/slice | solution.py:268
  228.2 3.8 slice.369
  237.9 4.3 fusion.11
  242.2 5.3 fusion.43
  247.6 4.1 multiply_reduce_fusion.6
  258.3 9.8 %fusion.35 = bf16[2,64,2048]{2,1,0:T(8,128)(2,1)} fusion(bf16[256,2,4,64]{0,3,2,1:T(8,128)(2,1)S(1)} %bitcast.342, f32[2,4,256,2048]{2,3,1,0:T(8,128)} %get-tuple-element.226, f32[2,4,256]{2,1,0:T(4,128)S(1)} %bitcast.373), kind=kOutput, calls=%fused_computation.65 | convolution fusion | flops 545521664 | bytes 17571840 | tf_op jit(solution)/shard_map/gqrl,rgqd->lgd/dot_general | solution.py:451
  268.0 13.0 %fusion = (f32[2,4,256]{2,1,0:T(4,128)S(1)}, f32[2,2048,256,4]{2,1,3,0:T(8,128)}) fusion(f32[2,4,256,2048]{2,3,1,0:T(8,128)} %get-tuple-element.226, f32[2,4,256]{2,1,0:T(4,128)S(1)} %bitcast.374, bf16[256,2,4,64]{0,3,2,1:T(8,128)(2,1)S(1)} %bitcast.343, bf16[2048,2,64,1]{0,2,1,3:T(8,128)(2,1)S(1)} %copy-done.45), kind=kOutput, calls=%fused_computation.2 | convolution fusion | flops 549451776 | bytes 34357248 | tf_op jit(solution)/shard_map/rgqd,lgd->gqrl/dot_general | solution.py:434
  281.5 7.8 %fusion.2 = bf16[2,4,256,2048]{2,3,1,0:T(8,128)(2,1)S(1)} fusion(f32[2,2048,256,4]{2,1,3,0:T(8,128)} %get-tuple-element.231, f32[2,4,256,2048]{2,3,1,0:T(8,128)S(1)} %bitcast.300, f32[2,4,256]{2,1,0:T(4,128)S(1)} %get-tuple-element.230, f32[2,4,256]{2,1,0:T(4,128)S(1)} %bitcast.375), kind=kLoop, calls=%fused_computation.4 | loop fusion | flops 16777216 | bytes 41959424 | tf_op jit(solution)/shard_map/convert_element_type | solution.py:438
  295.0 6.8 %fusion.38 = bf16[2,64,2048]{2,1,0:T(8,128)(2,1)} fusion(bf16[256,2,4,64]{0,3,2,1:T(8,128)(2,1)S(1)} %bitcast.345, bf16[2,4,256,2048]{2,3,1,0:T(8,128)(2,1)} %copy-done), kind=kOutput, calls=%fused_computation.66 | convolution fusion | flops 537395200 | bytes 9175040 | tf_op jit(solution)/shard_map/gqrl,rgqd->lgd/dot_general | solution.py:446
  325.3 4.2 collective-permute-start.15
  333.3 5.4 collective-permute-done.17
  346.4 5.4 fusion.88
  351.8 3.5 multiply_reduce_fusion.5
  364.2 3.9 fusion.30
  368.1 5.6 convert_add_fusion
  373.7 7.9 %reshape.585 = bf16[16,64,4,512]{3,2,1,0:T(4,128)(2,1)} reshape(bf16[1024,2048]{1,0:T(8,128)(2,1)} %convert_add_fusion) | data formatting | bytes 8388608 | tf_op jit(solution)/shard_map/reshape | solution.py:408
  381.5 3.5 copy.252
  385.1 3.9 pad_maximum_fusion
  389.7 5.4 fusion.14
  402.6 8.3 %collective-permute-done.23 = bf16[12,128,64]{1,2,0:T(8,128)(2,1)S(1)} collective-permute-done((bf16[12,128,64]{1,2,0:T(8,128)(2,1)S(1)}, bf16[12,128,64]{1,2,0:T(8,128)(2,1)S(1)}, u32[]{:S(2)}, u32[]{:S(2)}) %collective-permute-start.23) | collective-permute-done | bytes 196640 | tf_op jit(solution)/shard_map/ppermute | solution.py:40
  422.6 5.3 fusion.57
  443.4 4.0 fusion.169
  451.9 3.6 convolution_convert_fusion
  457.5 7.5 %collective-permute-done.36 = bf16[1024,2176]{1,0:T(8,128)(2,1)} collective-permute-done((bf16[1024,2176]{1,0:T(8,128)(2,1)}, bf16[1024,2176]{1,0:T(8,128)(2,1)}, u32[]{:S(2)}, u32[]{:S(2)}) %collective-permute-start.36) | collective-permute-done | bytes 4456480 | tf_op jit(solution)/shard_map/ppermute | solution.py:35
  465.0 6.2 %add_convert_fusion = bf16[1024,2176]{1,0:T(8,128)(2,1)} fusion(bf16[1024,2176]{1,0:T(8,128)(2,1)} %collective-permute-done.36, bf16[256,4352]{1,0:T(8,128)(2,1)} %copy-done.40, s32[]{:T(128)S(6)} %select_n.245, bf16[256,1024]{1,0:T(8,128)(2,1)S(1)} %copy-done.1, f32[1024]{0:T(1024)S(1)} %copy-done.71, f32[256]{0:T(256)S(1)} %copy-done.94), kind=kOutput, calls=%fused_computation.11 | convolution fusion | flops 1148583936 | bytes 10556420 | tf_op jit(solution)/shard_map/rk,rj->kj/dot_general | solution.py:208
  471.2 8.6 %all-to-all-start = ((bf16[64,16,2176]{2,1,0:T(8,128)(2,1)}), bf16[64,16,2176]{2,1,0:T(8,128)(2,1)}, u32[]{:S(2)}, u32[]{:S(2)}) async-start(bf16[64,16,2176]{2,1,0:T(8,128)(2,1)} %bitcast.301), calls=%async_computation | async-start | bytes 8912896 | tf_op jit(solution)/shard_map/all_to_all | solution.py:525
  480.2 7.9 %fusion.78 = (f32[1024]{0:T(1024)S(1)}, f32[256]{0:T(256)S(1)}, f32[256,1024]{1,0:T(8,128)}) fusion(bf16[256,1024]{1,0:T(8,128)(2,1)S(1)} %copy-done.1, f32[256]{0:T(256)S(1)} %copy-done.94, f32[1024]{0:T(1024)S(1)} %copy-done.71, bf16[256,4352]{1,0:T(8,128)(2,1)} %copy-done.40, bf16[1024,4352]{1,0:T(8,128)(2,1)} %all-gather.3.cloned.1.call-done), kind=kOutput, calls=%fused_computation.151 | convolution fusion | flops 2283535104 | bytes 12724224 | tf_op jit(solution)/shard_map/rj,kj->rk/dot_general | solution.py:212
  496.9 31.2 %collective-permute-done.28 = f32[96,128]{1,0:T(8,128)S(1)} collective-permute-done((f32[96,128]{1,0:T(8,128)S(1)}, f32[96,128]{1,0:T(8,128)S(1)}, u32[]{:S(2)}, u32[]{:S(2)}) %collective-permute-start.28) | collective-permute-done | bytes 49184 | tf_op jit(solution)/shard_map/ppermute | solution.py:40
  528.0 4.1 collective-permute-done.27
  532.1 5.9 collective-permute-start.32
  539.8 4.1 collective-permute-done.31
  548.8 3.5 all-to-all-start.2
  561.2 3.5 all-to-all-start.1
  567.2 8.2 %all-to-all-done.1 = bf16[8,16,2176]{2,1,0:T(8,128)(2,1)S(1)} async-done(((bf16[8,16,2176]{2,1,0:T(8,128)(2,1)}), bf16[8,16,2176]{2,1,0:T(8,128)(2,1)S(1)}, u32[]{:S(2)}, u32[]{:S(2)}) %all-to-all-start.1) | async-done | bytes 557088 | tf_op jit(solution)/shard_map/all_to_all | solution.py:72
  576.4 3.6 all-to-all-start.3
  584.3 11.6 %all-to-all-done.3 = bf16[8,128,512]{2,1,0:T(8,128)(2,1)S(1)} async-done(((bf16[8,128,512]{2,1,0:T(8,128)(2,1)}), bf16[8,128,512]{2,1,0:T(8,128)(2,1)S(1)}, u32[]{:S(2)}, u32[]{:S(2)}) %all-to-all-start.3) | async-done | bytes 1048608 | tf_op jit(solution)/shard_map/all_to_all | solution.py:72
  (575 shorter events, 229.4 us)
Async XLA Ops:
  7.3 78.9 %all-gather.3.cloned.1.call-start = ((), (), s32[]{:S(2)}) async-start(), calls=%async_computation.5 | async-start | bytes 8982528 | tf_op jit(solution)/shard_map/all_gather | solution.py:254
  13.1 203.7 %all-gather.5.cloned.1.call-start = ((), (), s32[]{:S(2)}) async-start(), calls=%async_computation.6 | async-start | bytes 16908288 | tf_op jit(solution)/shard_map/all_gather | solution.py:264
  14.8 534.1 %reduce-scatter.2.cloned.1.call-start = ((), (), s32[]{:S(2)}) async-start(), calls=%async_computation.7 | async-start | bytes 8912896 | tf_op jit(solution)/shard_map/reduce_scatter | solution.py:412
  14.9 5.8 collective-permute-start.5
  95.3 50.7 %collective-permute-start.1 = (bf16[264,256]{1,0:T(8,128)(2,1)}, bf16[264,256]{1,0:T(8,128)(2,1)}, u32[]{:S(2)}, u32[]{:S(2)}) collective-permute-start(bf16[264,256]{1,0:T(8,128)(2,1)} %get-tuple-element.200), channel_id=1, source_target_pairs={{0,4},{1,5},{2,6},{3,7},{4,0},{5,1},{6,2},{7,3},{8,12},{9,13},{10,... | collective-permute-start | bytes 405512 | tf_op jit(solution)/shard_map/ppermute | solution.py:40
  96.9 49.2 %collective-permute-start = (bf16[264,256]{1,0:T(8,128)(2,1)}, bf16[264,256]{1,0:T(8,128)(2,1)}, u32[]{:S(2)}, u32[]{:S(2)}) collective-permute-start(bf16[264,256]{1,0:T(8,128)(2,1)} %get-tuple-element.200), channel_id=1, source_target_pairs={{0,2},{1,3},{2,4},{3,5},{4,6},{5,7},{6,0},{7,1},{8,10},{9,11},{10,... | collective-permute-start | bytes 405512 | tf_op jit(solution)/shard_map/ppermute | solution.py:40
  97.4 48.7 %collective-permute-start.2 = (bf16[264,256]{1,0:T(8,128)(2,1)}, bf16[264,256]{1,0:T(8,128)(2,1)}, u32[]{:S(2)}, u32[]{:S(2)}) collective-permute-start(bf16[264,256]{1,0:T(8,128)(2,1)} %get-tuple-element.200), channel_id=1, source_target_pairs={{0,6},{1,7},{2,0},{3,1},{4,2},{5,3},{6,4},{7,5},{8,14},{9,15},{10,... | collective-permute-start | bytes 405512 | tf_op jit(solution)/shard_map/ppermute | solution.py:40
  101.9 30.8 %collective-permute-start.4 = (f32[3,1792]{1,0:T(4,128)}, f32[3,1792]{1,0:T(4,128)}, u32[]{:S(2)}, u32[]{:S(2)}) collective-permute-start(f32[3,1792]{1,0:T(4,128)} %slice.352), channel_id=1, source_target_pairs={{0,1},{1,2},{2,3},{3,4},{4,5},{5,6},{6,7},{8,9},{9,10},{10,11},{11... | collective-permute-start | bytes 64520 | tf_op jit(solution)/shard_map/ppermute | solution.py:30
  106.5 5.5 collective-permute-start.7
  113.8 5.0 collective-permute-start.11
  118.8 4.8 collective-permute-start.9
  123.6 5.0 collective-permute-start.22
  128.6 3.5 collective-permute-start.20
  145.7 4.4 collective-permute-start.6
  148.1 33.2 %collective-permute-start.3 = (bf16[4,264,256]{2,1,0:T(8,128)(2,1)}, bf16[4,264,256]{2,1,0:T(8,128)(2,1)}, u32[]{:S(2)}, u32[]{:S(2)}) collective-permute-start(bf16[4,264,256]{2,1,0:T(8,128)(2,1)} %pad_maximum_fusion.5), channel_id=1, source_target_pairs={{0,1},{1,0},{2,3},{3,2},{4,5},{5,4},{6,7},{7,6},{8,9},{9,8},{10,11... | collective-permute-start | bytes 1622024 | tf_op jit(solution)/shard_map/ppermute | solution.py:35
  150.2 12.0 %collective-permute-start.12 = (bf16[12,128,64]{1,2,0:T(8,128)(2,1)S(1)}, bf16[12,128,64]{1,2,0:T(8,128)(2,1)S(1)}, u32[]{:S(2)}, u32[]{:S(2)}) collective-permute-start(bf16[12,128,64]{1,2,0:T(8,128)(2,1)S(1)} %fusion.99), channel_id=1, source_target_pairs={{0,6},{1,7},{2,0},{3,1},{4,2},{5,3},{6,4},{7,5},{8,14},{9,15},{10,... | collective-permute-start | bytes 589832 | tf_op jit(solution)/shard_map/ppermute | solution.py:40
  151.0 13.4 %collective-permute-start.10 = (bf16[12,128,64]{1,2,0:T(8,128)(2,1)S(1)}, bf16[12,128,64]{1,2,0:T(8,128)(2,1)S(1)}, u32[]{:S(2)}, u32[]{:S(2)}) collective-permute-start(bf16[12,128,64]{1,2,0:T(8,128)(2,1)S(1)} %fusion.99), channel_id=1, source_target_pairs={{0,4},{1,5},{2,6},{3,7},{4,0},{5,1},{6,2},{7,3},{8,12},{9,13},{10,... | collective-permute-start | bytes 589832 | tf_op jit(solution)/shard_map/ppermute | solution.py:40
  151.6 17.5 %collective-permute-start.8 = (bf16[12,128,64]{1,2,0:T(8,128)(2,1)S(1)}, bf16[12,128,64]{1,2,0:T(8,128)(2,1)S(1)}, u32[]{:S(2)}, u32[]{:S(2)}) collective-permute-start(bf16[12,128,64]{1,2,0:T(8,128)(2,1)S(1)} %fusion.99), channel_id=1, source_target_pairs={{0,2},{1,3},{2,4},{3,5},{4,6},{5,7},{6,0},{7,1},{8,10},{9,11},{10,... | collective-permute-start | bytes 589832 | tf_op jit(solution)/shard_map/ppermute | solution.py:40
  169.5 2.0 collective-permute-start.13
  306.2 23.3 %collective-permute-start.37 = (bf16[512,512]{1,0:T(8,128)(2,1)}, bf16[512,512]{1,0:T(8,128)(2,1)}, u32[]{:S(2)}, u32[]{:S(2)}) collective-permute-start(bf16[512,512]{1,0:T(8,128)(2,1)} %convolution_convert_fusion.6), channel_id=1, source_target_pairs={{0,1},{1,0},{2,3},{3,2},{4,5},{5,4},{6,7},{7,6},{8,9},{9,8},{10,11... | collective-permute-start | bytes 1572872 | tf_op jit(solution)/shard_map/ppermute | solution.py:35
  309.5 51.4 %collective-permute-start.38 = (bf16[1536,512]{1,0:T(8,128)(2,1)}, bf16[1536,512]{1,0:T(8,128)(2,1)}, u32[]{:S(2)}, u32[]{:S(2)}) collective-permute-start(bf16[1536,512]{1,0:T(8,128)(2,1)} %convolution_convert_fusion.4), channel_id=1, source_target_pairs={{0,1},{1,0},{2,3},{3,2},{4,5},{5,4},{6,7},{7,6},{8,9},{9,8},{10,11... | collective-permute-start | bytes 4718600 | tf_op jit(solution)/shard_map/ppermute | solution.py:35
  313.0 55.0 %collective-permute-start.40 = (bf16[1024,2048]{1,0:T(8,128)(2,1)}, bf16[1024,2048]{1,0:T(8,128)(2,1)}, u32[]{:S(2)}, u32[]{:S(2)}) collective-permute-start(bf16[1024,2048]{1,0:T(8,128)(2,1)} %convolution_convert_fusion.1), channel_id=1, source_target_pairs={{0,1},{1,0},{2,3},{3,2},{4,5},{5,4},{6,7},{7,6},{8,9},{9,8},{10,11... | collective-permute-start | bytes 12582920 | tf_op jit(solution)/shard_map/ppermute | solution.py:35
  317.8 6.3 %collective-permute-start.14 = (bf16[4,256,256]{2,1,0:T(8,128)(2,1)}, bf16[4,256,256]{2,1,0:T(8,128)(2,1)}, u32[]{:S(2)}, u32[]{:S(2)}) collective-permute-start(bf16[4,256,256]{2,1,0:T(8,128)(2,1)} %bitcast.49), channel_id=1, source_target_pairs={{0,1},{1,0},{2,3},{3,2},{4,5},{5,4},{6,7},{7,6},{8,9},{9,8},{10,11... | collective-permute-start | bytes 1572872 | tf_op jit(solution)/shard_map/ppermute | solution.py:35
  325.3 7.8 %collective-permute-start.15 = (bf16[256,256]{1,0:T(8,128)(2,1)S(1)}, bf16[256,256]{1,0:T(8,128)(2,1)S(1)}, u32[]{:S(2)}, u32[]{:S(2)}) collective-permute-start(bf16[256,256]{1,0:T(8,128)(2,1)S(1)} %get-tuple-element.191), channel_id=1, source_target_pairs={{0,6},{1,7},{2,0},{3,1},{4,2},{5,3},{6,4},{7,5},{8,14},{9,15},{10,... | collective-permute-start | bytes 393224 | tf_op jit(solution)/shard_map/ppermute | solution.py:40
  329.5 9.3 %collective-permute-start.17 = (bf16[256,256]{1,0:T(8,128)(2,1)S(1)}, bf16[256,256]{1,0:T(8,128)(2,1)S(1)}, u32[]{:S(2)}, u32[]{:S(2)}) collective-permute-start(bf16[256,256]{1,0:T(8,128)(2,1)S(1)} %get-tuple-element.192), channel_id=1, source_target_pairs={{0,2},{1,3},{2,4},{3,5},{4,6},{5,7},{6,0},{7,1},{8,10},{9,11},{10,... | collective-permute-start | bytes 393224 | tf_op jit(solution)/shard_map/ppermute | solution.py:40
  329.5 9.3 %collective-permute-start.16 = (bf16[256,256]{1,0:T(8,128)(2,1)S(1)}, bf16[256,256]{1,0:T(8,128)(2,1)S(1)}, u32[]{:S(2)}, u32[]{:S(2)}) collective-permute-start(bf16[256,256]{1,0:T(8,128)(2,1)S(1)} %get-tuple-element.193), channel_id=1, source_target_pairs={{0,4},{1,5},{2,6},{3,7},{4,0},{5,1},{6,2},{7,3},{8,12},{9,13},{10,... | collective-permute-start | bytes 393224 | tf_op jit(solution)/shard_map/ppermute | solution.py:40
  333.2 31.0 %collective-permute-start.39 = (bf16[2048,512]{1,0:T(8,128)(2,1)}, bf16[2048,512]{1,0:T(8,128)(2,1)}, u32[]{:S(2)}, u32[]{:S(2)}) collective-permute-start(bf16[2048,512]{1,0:T(8,128)(2,1)} %convolution_convert_fusion.2), channel_id=1, source_target_pairs={{0,1},{1,0},{2,3},{3,2},{4,5},{5,4},{6,7},{7,6},{8,9},{9,8},{10,11... | collective-permute-start | bytes 6291464 | tf_op jit(solution)/shard_map/ppermute | solution.py:35
  360.8 37.3 %collective-permute-start.18 = (bf16[12,128,64]{1,2,0:T(8,128)(2,1)}, bf16[12,128,64]{1,2,0:T(8,128)(2,1)S(1)}, u32[]{:S(2)}, u32[]{:S(2)}) collective-permute-start(bf16[12,128,64]{1,2,0:T(8,128)(2,1)} %fusion.113), channel_id=1, source_target_pairs={{0,1},{1,0},{2,3},{3,2},{4,5},{5,4},{6,7},{7,6},{8,9},{9,8},{10,11... | collective-permute-start | bytes 589832 | tf_op jit(solution)/shard_map/ppermute | solution.py:35
  398.3 12.7 %collective-permute-start.23 = (bf16[12,128,64]{1,2,0:T(8,128)(2,1)S(1)}, bf16[12,128,64]{1,2,0:T(8,128)(2,1)S(1)}, u32[]{:S(2)}, u32[]{:S(2)}) collective-permute-start(bf16[12,128,64]{1,2,0:T(8,128)(2,1)S(1)} %fusion.101), channel_id=1, source_target_pairs={{0,2},{1,3},{2,4},{3,5},{4,6},{5,7},{6,0},{7,1},{8,10},{9,11},{10,... | collective-permute-start | bytes 589832 | tf_op jit(solution)/shard_map/ppermute | solution.py:40
  398.3 12.6 %collective-permute-start.21 = (bf16[12,128,64]{1,2,0:T(8,128)(2,1)S(1)}, bf16[12,128,64]{1,2,0:T(8,128)(2,1)S(1)}, u32[]{:S(2)}, u32[]{:S(2)}) collective-permute-start(bf16[12,128,64]{1,2,0:T(8,128)(2,1)S(1)} %fusion.101), channel_id=1, source_target_pairs={{0,4},{1,5},{2,6},{3,7},{4,0},{5,1},{6,2},{7,3},{8,12},{9,13},{10,... | collective-permute-start | bytes 589832 | tf_op jit(solution)/shard_map/ppermute | solution.py:40
  400.3 11.3 %collective-permute-start.19 = (bf16[12,128,64]{1,2,0:T(8,128)(2,1)S(1)}, bf16[12,128,64]{1,2,0:T(8,128)(2,1)S(1)}, u32[]{:S(2)}, u32[]{:S(2)}) collective-permute-start(bf16[12,128,64]{1,2,0:T(8,128)(2,1)S(1)} %fusion.101), channel_id=1, source_target_pairs={{0,6},{1,7},{2,0},{3,1},{4,2},{5,3},{6,4},{7,5},{8,14},{9,15},{10,... | collective-permute-start | bytes 589832 | tf_op jit(solution)/shard_map/ppermute | solution.py:40
  412.8 1.7 collective-permute-start.24
  448.3 3.4 collective-permute-start.25
  455.5 9.5 %collective-permute-start.36 = (bf16[1024,2176]{1,0:T(8,128)(2,1)}, bf16[1024,2176]{1,0:T(8,128)(2,1)}, u32[]{:S(2)}, u32[]{:S(2)}) collective-permute-start(bf16[1024,2176]{1,0:T(8,128)(2,1)} %convolution_convert_fusion), channel_id=1, source_target_pairs={{0,1},{1,0},{2,3},{3,2},{4,5},{5,4},{6,7},{7,6},{8,9},{9,8},{10,11... | collective-permute-start | bytes 13369352 | tf_op jit(solution)/shard_map/ppermute | solution.py:35
  471.2 77.6 %all-to-all-start = ((bf16[64,16,2176]{2,1,0:T(8,128)(2,1)}), bf16[64,16,2176]{2,1,0:T(8,128)(2,1)}, u32[]{:S(2)}, u32[]{:S(2)}) async-start(bf16[64,16,2176]{2,1,0:T(8,128)(2,1)} %bitcast.301), calls=%async_computation | async-start | bytes 8912896 | tf_op jit(solution)/shard_map/all_to_all | solution.py:525
  488.2 1.3 collective-permute-start.26
  489.5 38.5 %collective-permute-start.28 = (f32[96,128]{1,0:T(8,128)S(1)}, f32[96,128]{1,0:T(8,128)S(1)}, u32[]{:S(2)}, u32[]{:S(2)}) collective-permute-start(f32[96,128]{1,0:T(8,128)S(1)} %fusion.161), channel_id=1, source_target_pairs={{0,2},{1,3},{2,4},{3,5},{4,6},{5,7},{6,0},{7,1},{8,10},{9,11},{10,... | collective-permute-start | bytes 147464 | tf_op jit(solution)/shard_map/ppermute | solution.py:40
  491.3 36.7 %collective-permute-start.29 = (f32[96,128]{1,0:T(8,128)S(1)}, f32[96,128]{1,0:T(8,128)S(1)}, u32[]{:S(2)}, u32[]{:S(2)}) collective-permute-start(f32[96,128]{1,0:T(8,128)S(1)} %fusion.161), channel_id=1, source_target_pairs={{0,6},{1,7},{2,0},{3,1},{4,2},{5,3},{6,4},{7,5},{8,14},{9,15},{10,... | collective-permute-start | bytes 147464 | tf_op jit(solution)/shard_map/ppermute | solution.py:40
  492.8 39.3 %collective-permute-start.27 = (f32[96,128]{1,0:T(8,128)S(1)}, f32[96,128]{1,0:T(8,128)S(1)}, u32[]{:S(2)}, u32[]{:S(2)}) collective-permute-start(f32[96,128]{1,0:T(8,128)S(1)} %fusion.161), channel_id=1, source_target_pairs={{0,4},{1,5},{2,6},{3,7},{4,0},{5,1},{6,2},{7,3},{8,12},{9,13},{10,... | collective-permute-start | bytes 147464 | tf_op jit(solution)/shard_map/ppermute | solution.py:40
  532.1 7.7 %collective-permute-start.32 = (f32[96,128]{1,0:T(8,128)S(1)}, f32[96,128]{1,0:T(8,128)S(1)}, u32[]{:S(2)}, u32[]{:S(2)}) collective-permute-start(f32[96,128]{1,0:T(8,128)S(1)} %add_add_fusion.4), channel_id=1, source_target_pairs={{0,24},{8,0},{16,8},{24,16},{32,56},{40,32},{48,40},{56,48},{64,88... | collective-permute-start | bytes 147464 | tf_op jit(solution)/shard_map/ppermute | solution.py:50
  538.0 5.8 collective-permute-start.31
  538.0 5.8 collective-permute-start.30
  543.9 10.9 %collective-permute-start.35 = (f32[96,128]{1,0:T(8,128)S(1)}, f32[96,128]{1,0:T(8,128)S(1)}, u32[]{:S(2)}, u32[]{:S(2)}) collective-permute-start(f32[96,128]{1,0:T(8,128)S(1)} %add_add_fusion.3), channel_id=1, source_target_pairs={{0,96},{8,104},{16,112},{24,120},{32,0},{40,8},{48,16},{56,24},{64... | collective-permute-start | bytes 147464 | tf_op jit(solution)/shard_map/ppermute | solution.py:50
  546.7 8.1 %collective-permute-start.34 = (f32[96,128]{1,0:T(8,128)S(1)}, f32[96,128]{1,0:T(8,128)S(1)}, u32[]{:S(2)}, u32[]{:S(2)}) collective-permute-start(f32[96,128]{1,0:T(8,128)S(1)} %add_add_fusion.3), channel_id=1, source_target_pairs={{0,32},{8,40},{16,48},{24,56},{32,64},{40,72},{48,80},{56,88},{64,... | collective-permute-start | bytes 147464 | tf_op jit(solution)/shard_map/ppermute | solution.py:50
  546.7 8.1 %collective-permute-start.33 = (f32[96,128]{1,0:T(8,128)S(1)}, f32[96,128]{1,0:T(8,128)S(1)}, u32[]{:S(2)}, u32[]{:S(2)}) collective-permute-start(f32[96,128]{1,0:T(8,128)S(1)} %add_add_fusion.3), channel_id=1, source_target_pairs={{0,64},{8,72},{16,80},{24,88},{32,96},{40,104},{48,112},{56,120},{... | collective-permute-start | bytes 147464 | tf_op jit(solution)/shard_map/ppermute | solution.py:50
  548.8 11.5 %all-to-all-start.2 = ((bf16[4,128,512]{2,1,0:T(8,128)(2,1)}), bf16[4,128,512]{2,1,0:T(8,128)(2,1)S(1)}, u32[]{:S(2)}, u32[]{:S(2)}) async-start(bf16[4,128,512]{2,1,0:T(8,128)(2,1)} %bitcast.364), calls=%async_computation.3 | async-start | bytes 1048576 | tf_op jit(solution)/shard_map/all_to_all | solution.py:415
  561.2 14.2 %all-to-all-start.1 = ((bf16[8,16,2176]{2,1,0:T(8,128)(2,1)}), bf16[8,16,2176]{2,1,0:T(8,128)(2,1)S(1)}, u32[]{:S(2)}, u32[]{:S(2)}) async-start(bf16[8,16,2176]{2,1,0:T(8,128)(2,1)} %broadcast_in_dim.59), calls=%async_computation.1 | async-start | bytes 1114112 | tf_op jit(solution)/shard_map/all_to_all | solution.py:72
  576.4 19.4 %all-to-all-start.3 = ((bf16[8,128,512]{2,1,0:T(8,128)(2,1)}), bf16[8,128,512]{2,1,0:T(8,128)(2,1)S(1)}, u32[]{:S(2)}, u32[]{:S(2)}) async-start(bf16[8,128,512]{2,1,0:T(8,128)(2,1)} %broadcast_in_dim.60), calls=%async_computation.4 | async-start | bytes 2097152 | tf_op jit(solution)/shard_map/all_to_all | solution.py:72
  (143 other events, 1786.8 us)
Sparse Core Ops, SparseCore 0:
  13.2 72.8 all-gather.2
  89.8 86.2 all-gather.4
  389.1 82.2 reduce-scatter.1
